TPU v7x, 256 devices: a whole 4x4x8 slice. The times are simulated.
256 devices in a mesh: section: 4 (over z_lo), dp: 64 (over z_hi, y, x, core).
Axes of the slice: x: 4, y: 4, z: 8 (z_hi: 2, z_lo: 4; z = z_hi * 4 + z_lo), core: 2. Of those that a mesh axis runs over, the one named last changes fastest.
Arguments:
- images: bfloat16 [4, 64, 16, 16, 320], P(None, 'dp'), may hold values from -6 to 6
- cotangent: bfloat16 [4, 64, 16, 16, 320], P(None, 'dp'), may hold values from -6 to 6
- heights: int32 [4], replicated, may hold values from 8 to 16, as said below
- dw_kernel: float32 [2, 4, 7, 7, 320], P(None, 'section'), may hold values from -0.875 to 0.875
- dw_bias: float32 [2, 4, 320], P(None, 'section'), may hold values from -1 to 1
- norm_gain: float32 [2, 4, 320], P(None, 'section'), may hold values from 0.5 to 1.5
- norm_bias: float32 [2, 4, 320], P(None, 'section'), may hold values from -3 to 3
- up_weight: bfloat16 [2, 4, 320, 1280], P(None, 'section'), may hold values from -0.3125 to 0.3125
- up_bias: float32 [2, 4, 1280], P(None, 'section'), may hold values from -3 to 3
- down_weight: bfloat16 [2, 4, 1280, 320], P(None, 'section'), may hold values from -0.15625 to 0.15625
- down_bias: float32 [2, 4, 320], P(None, 'section'), may hold values from -3 to 3
- layer_scale: float32 [2, 4, 320], P(None, 'section'), may hold values from 0.1 to 1
Outputs:
- grad_dw_kernel: float32 [2, 4, 7, 7, 320], P(None, 'section')
- grad_dw_bias: float32 [2, 4, 320], P(None, 'section')
- grad_norm_gain: float32 [2, 4, 320], P(None, 'section')
- grad_norm_bias: float32 [2, 4, 320], P(None, 'section')
- grad_up_weight: bfloat16 [2, 4, 320, 1280], P(None, 'section')
- grad_up_bias: float32 [2, 4, 1280], P(None, 'section')
- grad_down_weight: bfloat16 [2, 4, 1280, 320], P(None, 'section')
- grad_down_bias: float32 [2, 4, 320], P(None, 'section')
- grad_layer_scale: float32 [2, 4, 320], P(None, 'section')
Inputs may be any that keep to these rules, and one draw needn't show every extreme that they name: heights[m] is one of 8, 12 and 16; some micro-batch has 16.
All inputs are finite; a program needn't handle non-finite values.
Results may differ from a plain program's by a relative error of at most 0.025.
Values may be sent and summed in bfloat16 or wider, within the bound.
A program may use at most 128 MiB of HBM per device.

v0:
```python
import jax
import jax.numpy as jnp
from jax import lax
from jax.sharding import PartitionSpec as P


def shifted_2(value, axis, steps):
    count = lax.axis_size(axis)
    pairs = [(source, (source + steps) % count) for source in range(count)]
    return lax.ppermute(value, axis, pairs)


def make_window(height, side):
    rows = lax.iota(jnp.int32, side)
    inside = (rows < height).astype(jnp.float32)
    return inside[:, None] * inside[None, :]


def block_apply(params, inputs, window):
    (
        dw_kernel,
        dw_bias,
        norm_gain,
        norm_bias,
        up_weight,
        up_bias,
        down_weight,
        down_bias,
        layer_scale,
    ) = params
    side = inputs.shape[0]
    width = inputs.shape[2]
    widened = inputs.astype(jnp.float32)
    padded = jnp.pad(widened, ((3, 3), (3, 3), (0, 0)))
    mixed = jnp.zeros_like(widened) + dw_bias
    for row_off in range(7):
        for col_off in range(7):
            mixed = (
                mixed
                + padded[row_off : row_off + side, col_off : col_off + side]
                * dw_kernel[row_off, col_off]
            )
    center = jnp.mean(mixed, axis=-1, keepdims=True)
    spread = jnp.mean((mixed - center) ** 2, axis=-1, keepdims=True)
    normed = ((mixed - center) * lax.rsqrt(spread + 1e-06) * norm_gain + norm_bias).astype(
        jnp.bfloat16
    )
    flat = normed.reshape(side * side, width)
    hidden = jnp.dot(flat, up_weight, preferred_element_type=jnp.float32) + up_bias
    active = jax.nn.gelu(hidden, approximate=True).astype(jnp.bfloat16)
    projected = jnp.dot(active, down_weight, preferred_element_type=jnp.float32) + down_bias
    result = (widened + layer_scale * projected.reshape(side, side, width)) * window[:, :, None]
    return result.astype(jnp.bfloat16)


def body(
    images,
    cotangent,
    heights,
    dw_kernel,
    dw_bias,
    norm_gain,
    norm_bias,
    up_weight,
    up_bias,
    down_weight,
    down_bias,
    layer_scale,
):
    sections = lax.axis_size("section")
    place = lax.axis_index("section")
    micros = images.shape[0]
    side = images.shape[2]
    loops = dw_kernel.shape[0]
    weights = tuple(
        (
            a[:, 0]
            for a in (
                dw_kernel,
                dw_bias,
                norm_gain,
                norm_bias,
                up_weight,
                up_bias,
                down_weight,
                down_bias,
                layer_scale,
            )
        )
    )
    ticks = loops * sections + micros - 1

    def locate(tick, offset):
        shifted = tick - offset
        loop_no = shifted // sections
        micro = shifted % sections
        valid = (shifted >= 0) & (micro < micros) & (loop_no < loops)
        return (jnp.clip(loop_no, 0, loops - 1), jnp.clip(micro, 0, micros - 1), valid)

    def forward_tick(tick, carry):
        held, stash = carry
        loop_no, micro, valid = locate(tick, place)
        window = make_window(heights[micro], side)
        fresh = (images[micro, 0].astype(jnp.float32) * window[:, :, None]).astype(jnp.bfloat16)
        start = jnp.where((place == 0) & (loop_no == 0), fresh, held)
        stash = stash.at[loop_no, micro].set(jnp.where(valid, start, stash[loop_no, micro]))
        params = tuple((a[loop_no] for a in weights))
        result = lax.cond(
            valid, lambda: block_apply(params, start, window), lambda: jnp.zeros_like(start)
        )
        held = shifted_2(result, "section", 1)
        return (held, stash)

    blank = jnp.zeros(images.shape[2:], jnp.bfloat16)
    stash0 = jnp.zeros((loops, micros) + images.shape[2:], jnp.bfloat16)
    unused_held, stash = lax.fori_loop(0, ticks, forward_tick, (blank, stash0))

    def backward_tick(tick, carry):
        held, totals = carry
        loop_rev, micro, valid = locate(tick, sections - 1 - place)
        loop_no = loops - 1 - loop_rev
        window = make_window(heights[micro], side)
        incoming = jnp.where((place == sections - 1) & (loop_rev == 0), cotangent[micro, 0], held)
        inputs = stash[loop_no, micro]
        params = tuple((a[loop_no] for a in weights))

        def working():
            unused, pullback = jax.vjp(lambda p, v: block_apply(p, v, window), params, inputs)
            dparams, dinputs = pullback(incoming)
            return (dinputs, tuple((g.astype(jnp.float32) for g in dparams)))

        def resting():
            return (
                jnp.zeros_like(inputs),
                tuple((jnp.zeros(a.shape, jnp.float32) for a in params)),
            )

        dinputs, grads = lax.cond(valid, working, resting)
        totals = tuple((t.at[loop_no].add(g) for t, g in zip(totals, grads)))
        held = shifted_2(dinputs, "section", -1)
        return (held, totals)

    zeros = tuple((jnp.zeros(a.shape, jnp.float32) for a in weights))
    unused_grad, totals = lax.fori_loop(0, ticks, backward_tick, (blank, zeros))
    summed = lax.psum(totals, "dp")
    shaped = [s[:, None] for s in summed]
    shaped[4] = shaped[4].astype(jnp.bfloat16)
    shaped[6] = shaped[6].astype(jnp.bfloat16)
    return (
        shaped[0],
        shaped[1],
        shaped[2],
        shaped[3],
        shaped[4],
        shaped[5],
        shaped[6],
        shaped[7],
        shaped[8],
    )


def solution(mesh):
    in_specs = (
        P(None, "dp", None, None, None),
        P(None, "dp", None, None, None),
        P(),
        P(None, "section", None, None, None),
        P(None, "section", None),
        P(None, "section", None),
        P(None, "section", None),
        P(None, "section", None, None),
        P(None, "section", None),
        P(None, "section", None, None),
        P(None, "section", None),
        P(None, "section", None),
    )
    out_specs = (
        P(None, "section", None, None, None),
        P(None, "section", None),
        P(None, "section", None),
        P(None, "section", None),
        P(None, "section", None, None),
        P(None, "section", None),
        P(None, "section", None, None),
        P(None, "section", None),
        P(None, "section", None),
    )
    return jax.shard_map(body, mesh=mesh, in_specs=in_specs, out_specs=out_specs, check_vma=False)
```

profile of v0, /device:TPU:1, one launch (start us, length us, event | category | flops | bytes accessed | tf_op | source)
XLA Modules:
  0.0 1699.0 jit_solution(17061309103286432854)
XLA Ops:
  13.8 208.4 %while.60 = (s32[]{:T(128)}, bf16[16,16,320]{2,1,0:T(8,128)(2,1)S(1)}, bf16[2,4,16,16,320]{4,3,2,1,0:T(8,128)(2,1)}, s32[]{:T(128)}, pred[]{:T(512)}, /*index=5*...) while((s32[]{:T(128)}, ...), condition=%wide.region_6.7_spmd, body=%wide.region_0.6_spmd.sunk | while | flops 432538464 | bytes 7803341 | solution.py:116
  19.3 7.8 conditional.4
  38.9 7.8 conditional.4
  58.5 7.8 conditional.4
  78.1 7.8 conditional.4
  97.7 7.8 conditional.4
  136.9 7.8 conditional.4
  156.5 7.8 conditional.4
  192.3 12.2 collective-permute-done
  210.0 12.2 collective-permute-done
  230.3 719.7 %while.61 = (s32[]{:T(128)}, bf16[16,16,320]{2,1,0:T(8,128)(2,1)S(1)}, f32[2,7,7,320]{3,0,2,1:T(2,128)}, f32[2,320]{1,0:T(2,128)}, f32[2,320]{1,0:T(2,128)}, /*i...) while((s32[]{:T(128)}, ...), condition=%wide.region_73.74_spmd, body=%wide.region_7.73_spmd.sunk | while | flops 1306038272 | bytes 83926840 | solution.py:144
  235.4 34.0 %collective-permute-start.1 = (bf16[16,16,320]{2,1,0:T(8,128)(2,1)}, bf16[16,16,320]{2,1,0:T(8,128)(2,1)S(1)}, u32[]{:S(2)}, u32[]{:S(2)}) collective-permute-start(bf16[16,16,320]{2,1,0:T(8,128)(2,1)} %get-tuple-element.2207), channel_id=1, source_target_pairs={{0,192},{64,0},{128,64},{192,128},{1,193},{65,1},{129,65},{193,129... | collective-permute-start | bytes 491528 | tf_op jit(solution)/shard_map/while/body/eval_jaxpr/ppermute | solution.py:10
  301.9 32.5 %collective-permute-start.1 = (bf16[16,16,320]{2,1,0:T(8,128)(2,1)}, bf16[16,16,320]{2,1,0:T(8,128)(2,1)S(1)}, u32[]{:S(2)}, u32[]{:S(2)}) collective-permute-start(bf16[16,16,320]{2,1,0:T(8,128)(2,1)} %get-tuple-element.2207), channel_id=1, source_target_pairs={{0,192},{64,0},{128,64},{192,128},{1,193},{65,1},{129,65},{193,129... | collective-permute-start | bytes 491528 | tf_op jit(solution)/shard_map/while/body/eval_jaxpr/ppermute | solution.py:10
  366.8 32.5 %collective-permute-start.1 = (bf16[16,16,320]{2,1,0:T(8,128)(2,1)}, bf16[16,16,320]{2,1,0:T(8,128)(2,1)S(1)}, u32[]{:S(2)}, u32[]{:S(2)}) collective-permute-start(bf16[16,16,320]{2,1,0:T(8,128)(2,1)} %get-tuple-element.2207), channel_id=1, source_target_pairs={{0,192},{64,0},{128,64},{192,128},{1,193},{65,1},{129,65},{193,129... | collective-permute-start | bytes 491528 | tf_op jit(solution)/shard_map/while/body/eval_jaxpr/ppermute | solution.py:10
  429.6 34.6 %conditional.5 = (bf16[16,16,320]{2,1,0:T(8,128)(2,1)}, f32[1,7,7,320]{3,2,1,0:T(8,128)S(1)}, f32[1,320]{1,0:T(1,128)S(1)}, f32[1,320]{1,0:T(1,128)S(1)}, f32[1,...) conditional(s32[]{:T(128)} %convert_element_type.261, ...), branch_computations={%region_8.8_spmd, %region_9.69_spmd} | conditional | flops 1304362624 | bytes 72641240 | solution.py:138
  494.6 34.6 %conditional.5 = (bf16[16,16,320]{2,1,0:T(8,128)(2,1)}, f32[1,7,7,320]{3,2,1,0:T(8,128)S(1)}, f32[1,320]{1,0:T(1,128)S(1)}, f32[1,320]{1,0:T(1,128)S(1)}, f32[1,...) conditional(s32[]{:T(128)} %convert_element_type.261, ...), branch_computations={%region_8.8_spmd, %region_9.69_spmd} | conditional | flops 1304362624 | bytes 72641240 | solution.py:138
  559.6 34.6 %conditional.5 = (bf16[16,16,320]{2,1,0:T(8,128)(2,1)}, f32[1,7,7,320]{3,2,1,0:T(8,128)S(1)}, f32[1,320]{1,0:T(1,128)S(1)}, f32[1,320]{1,0:T(1,128)S(1)}, f32[1,...) conditional(s32[]{:T(128)} %convert_element_type.261, ...), branch_computations={%region_8.8_spmd, %region_9.69_spmd} | conditional | flops 1304362624 | bytes 72641240 | solution.py:138
  624.6 34.6 %conditional.5 = (bf16[16,16,320]{2,1,0:T(8,128)(2,1)}, f32[1,7,7,320]{3,2,1,0:T(8,128)S(1)}, f32[1,320]{1,0:T(1,128)S(1)}, f32[1,320]{1,0:T(1,128)S(1)}, f32[1,...) conditional(s32[]{:T(128)} %convert_element_type.261, ...), branch_computations={%region_8.8_spmd, %region_9.69_spmd} | conditional | flops 1304362624 | bytes 72641240 | solution.py:138
  693.3 34.6 %conditional.5 = (bf16[16,16,320]{2,1,0:T(8,128)(2,1)}, f32[1,7,7,320]{3,2,1,0:T(8,128)S(1)}, f32[1,320]{1,0:T(1,128)S(1)}, f32[1,320]{1,0:T(1,128)S(1)}, f32[1,...) conditional(s32[]{:T(128)} %convert_element_type.261, ...), branch_computations={%region_8.8_spmd, %region_9.69_spmd} | conditional | flops 1304362624 | bytes 72641240 | solution.py:138
  758.2 34.6 %conditional.5 = (bf16[16,16,320]{2,1,0:T(8,128)(2,1)}, f32[1,7,7,320]{3,2,1,0:T(8,128)S(1)}, f32[1,320]{1,0:T(1,128)S(1)}, f32[1,320]{1,0:T(1,128)S(1)}, f32[1,...) conditional(s32[]{:T(128)} %convert_element_type.261, ...), branch_computations={%region_8.8_spmd, %region_9.69_spmd} | conditional | flops 1304362624 | bytes 72641240 | solution.py:138
  823.2 34.6 %conditional.5 = (bf16[16,16,320]{2,1,0:T(8,128)(2,1)}, f32[1,7,7,320]{3,2,1,0:T(8,128)S(1)}, f32[1,320]{1,0:T(1,128)S(1)}, f32[1,320]{1,0:T(1,128)S(1)}, f32[1,...) conditional(s32[]{:T(128)} %convert_element_type.261, ...), branch_computations={%region_8.8_spmd, %region_9.69_spmd} | conditional | flops 1304362624 | bytes 72641240 | solution.py:138
  888.1 34.6 %conditional.5 = (bf16[16,16,320]{2,1,0:T(8,128)(2,1)}, f32[1,7,7,320]{3,2,1,0:T(8,128)S(1)}, f32[1,320]{1,0:T(1,128)S(1)}, f32[1,320]{1,0:T(1,128)S(1)}, f32[1,...) conditional(s32[]{:T(128)} %convert_element_type.261, ...), branch_computations={%region_8.8_spmd, %region_9.69_spmd} | conditional | flops 1304362624 | bytes 72641240 | solution.py:138
  954.2 460.4 %all-reduce.105 = (f32[2,1,320]{2,1,0:T(1,128)}, f32[2,1,320]{2,1,0:T(1,128)}, f32[2,1,320]{2,1,0:T(1,128)}, bf16[2,320,1280]{2,1,0:T(8,128)(2,1)}, f32[2,1,1280...) all-reduce(f32[2,1,320]{2,1,0:T(1,128)S(1)} %broadcast_in_dim.194, ...), channel_id=1, replica_groups=mesh['section'=4,'dp'=64] {'dp'}, use_global_device_ids=true, to_apply=%region_75.76 | all-reduce | flops 1644160 | bytes 9876480 | tf_op jit(solution)/shard_map/psum | solution.py:145
  1414.5 275.8 %all-reduce.104.cloned.1.call-done = f32[2,1,7,7,320]{4,0,3,2,1:T(2,128)} async-done(((f32[2,1,7,7,320]{4,0,3,2,1:T(2,128)}), f32[2,1,7,7,320]{4,0,3,2,1:T(2,128)}) %all-reduce.104.cloned.1.call-update) | async-done | bytes 125456 | tf_op jit(solution)/shard_map/psum | solution.py:145
  (3088 shorter events, 821.2 us)
Async XLA Ops:
  7.2 1683.2 %all-reduce.104.cloned.1.call-start = ((), (), s32[]{:S(2)}) async-start(), calls=%async_computation | async-start | bytes 301056 | tf_op jit(solution)/shard_map/psum | solution.py:145
  27.1 6.4 collective-permute-start
  46.7 6.4 collective-permute-start
  66.3 6.4 collective-permute-start
  85.9 6.4 collective-permute-start
  105.5 6.4 collective-permute-start
  125.1 6.4 collective-permute-start
  144.7 6.4 collective-permute-start
  164.3 6.4 collective-permute-start
  176.2 10.4 collective-permute-start
  192.1 12.3 collective-permute-start
  209.9 12.3 collective-permute-start
  235.4 46.9 %copy-start.88 = (f32[1,320]{1,0:T(1,128)}, f32[1,320]{1,0:T(1,128)S(1)}, u32[]{:S(2)}) copy-start(f32[1,320]{1,0:T(1,128)S(1)} %get-tuple-element.2209) | copy-start | bytes 3844 | tf_op jit(solution)/shard_map/while
  235.4 60.6 %collective-permute-start.1 = (bf16[16,16,320]{2,1,0:T(8,128)(2,1)}, bf16[16,16,320]{2,1,0:T(8,128)(2,1)S(1)}, u32[]{:S(2)}, u32[]{:S(2)}) collective-permute-start(bf16[16,16,320]{2,1,0:T(8,128)(2,1)} %get-tuple-element.2207), channel_id=1, source_target_pairs={{0,192},{64,0},{128,64},{192,128},{1,193},{65,1},{129,65},{193,129... | collective-permute-start | bytes 491528 | tf_op jit(solution)/shard_map/while/body/eval_jaxpr/ppermute | solution.py:10
  301.9 59.2 %collective-permute-start.1 = (bf16[16,16,320]{2,1,0:T(8,128)(2,1)}, bf16[16,16,320]{2,1,0:T(8,128)(2,1)S(1)}, u32[]{:S(2)}, u32[]{:S(2)}) collective-permute-start(bf16[16,16,320]{2,1,0:T(8,128)(2,1)} %get-tuple-element.2207), channel_id=1, source_target_pairs={{0,192},{64,0},{128,64},{192,128},{1,193},{65,1},{129,65},{193,129... | collective-permute-start | bytes 491528 | tf_op jit(solution)/shard_map/while/body/eval_jaxpr/ppermute | solution.py:10
  366.8 59.1 %collective-permute-start.1 = (bf16[16,16,320]{2,1,0:T(8,128)(2,1)}, bf16[16,16,320]{2,1,0:T(8,128)(2,1)S(1)}, u32[]{:S(2)}, u32[]{:S(2)}) collective-permute-start(bf16[16,16,320]{2,1,0:T(8,128)(2,1)} %get-tuple-element.2207), channel_id=1, source_target_pairs={{0,192},{64,0},{128,64},{192,128},{1,193},{65,1},{129,65},{193,129... | collective-permute-start | bytes 491528 | tf_op jit(solution)/shard_map/while/body/eval_jaxpr/ppermute | solution.py:10
  464.2 26.7 %collective-permute-start.1 = (bf16[16,16,320]{2,1,0:T(8,128)(2,1)}, bf16[16,16,320]{2,1,0:T(8,128)(2,1)S(1)}, u32[]{:S(2)}, u32[]{:S(2)}) collective-permute-start(bf16[16,16,320]{2,1,0:T(8,128)(2,1)} %get-tuple-element.2207), channel_id=1, source_target_pairs={{0,192},{64,0},{128,64},{192,128},{1,193},{65,1},{129,65},{193,129... | collective-permute-start | bytes 491528 | tf_op jit(solution)/shard_map/while/body/eval_jaxpr/ppermute | solution.py:10
  529.2 26.7 %collective-permute-start.1 = (bf16[16,16,320]{2,1,0:T(8,128)(2,1)}, bf16[16,16,320]{2,1,0:T(8,128)(2,1)S(1)}, u32[]{:S(2)}, u32[]{:S(2)}) collective-permute-start(bf16[16,16,320]{2,1,0:T(8,128)(2,1)} %get-tuple-element.2207), channel_id=1, source_target_pairs={{0,192},{64,0},{128,64},{192,128},{1,193},{65,1},{129,65},{193,129... | collective-permute-start | bytes 491528 | tf_op jit(solution)/shard_map/while/body/eval_jaxpr/ppermute | solution.py:10
  594.2 26.7 %collective-permute-start.1 = (bf16[16,16,320]{2,1,0:T(8,128)(2,1)}, bf16[16,16,320]{2,1,0:T(8,128)(2,1)S(1)}, u32[]{:S(2)}, u32[]{:S(2)}) collective-permute-start(bf16[16,16,320]{2,1,0:T(8,128)(2,1)} %get-tuple-element.2207), channel_id=1, source_target_pairs={{0,192},{64,0},{128,64},{192,128},{1,193},{65,1},{129,65},{193,129... | collective-permute-start | bytes 491528 | tf_op jit(solution)/shard_map/while/body/eval_jaxpr/ppermute | solution.py:10
  659.1 30.5 %collective-permute-start.1 = (bf16[16,16,320]{2,1,0:T(8,128)(2,1)}, bf16[16,16,320]{2,1,0:T(8,128)(2,1)S(1)}, u32[]{:S(2)}, u32[]{:S(2)}) collective-permute-start(bf16[16,16,320]{2,1,0:T(8,128)(2,1)} %get-tuple-element.2207), channel_id=1, source_target_pairs={{0,192},{64,0},{128,64},{192,128},{1,193},{65,1},{129,65},{193,129... | collective-permute-start | bytes 491528 | tf_op jit(solution)/shard_map/while/body/eval_jaxpr/ppermute | solution.py:10
  727.9 26.7 %collective-permute-start.1 = (bf16[16,16,320]{2,1,0:T(8,128)(2,1)}, bf16[16,16,320]{2,1,0:T(8,128)(2,1)S(1)}, u32[]{:S(2)}, u32[]{:S(2)}) collective-permute-start(bf16[16,16,320]{2,1,0:T(8,128)(2,1)} %get-tuple-element.2207), channel_id=1, source_target_pairs={{0,192},{64,0},{128,64},{192,128},{1,193},{65,1},{129,65},{193,129... | collective-permute-start | bytes 491528 | tf_op jit(solution)/shard_map/while/body/eval_jaxpr/ppermute | solution.py:10
  792.8 26.7 %collective-permute-start.1 = (bf16[16,16,320]{2,1,0:T(8,128)(2,1)}, bf16[16,16,320]{2,1,0:T(8,128)(2,1)S(1)}, u32[]{:S(2)}, u32[]{:S(2)}) collective-permute-start(bf16[16,16,320]{2,1,0:T(8,128)(2,1)} %get-tuple-element.2207), channel_id=1, source_target_pairs={{0,192},{64,0},{128,64},{192,128},{1,193},{65,1},{129,65},{193,129... | collective-permute-start | bytes 491528 | tf_op jit(solution)/shard_map/while/body/eval_jaxpr/ppermute | solution.py:10
  857.8 26.7 %collective-permute-start.1 = (bf16[16,16,320]{2,1,0:T(8,128)(2,1)}, bf16[16,16,320]{2,1,0:T(8,128)(2,1)S(1)}, u32[]{:S(2)}, u32[]{:S(2)}) collective-permute-start(bf16[16,16,320]{2,1,0:T(8,128)(2,1)} %get-tuple-element.2207), channel_id=1, source_target_pairs={{0,192},{64,0},{128,64},{192,128},{1,193},{65,1},{129,65},{193,129... | collective-permute-start | bytes 491528 | tf_op jit(solution)/shard_map/while/body/eval_jaxpr/ppermute | solution.py:10
  922.7 26.7 %collective-permute-start.1 = (bf16[16,16,320]{2,1,0:T(8,128)(2,1)}, bf16[16,16,320]{2,1,0:T(8,128)(2,1)S(1)}, u32[]{:S(2)}, u32[]{:S(2)}) collective-permute-start(bf16[16,16,320]{2,1,0:T(8,128)(2,1)} %get-tuple-element.2207), channel_id=1, source_target_pairs={{0,192},{64,0},{128,64},{192,128},{1,193},{65,1},{129,65},{193,129... | collective-permute-start | bytes 491528 | tf_op jit(solution)/shard_map/while/body/eval_jaxpr/ppermute | solution.py:10
  (874 other events, 3704.1 us)
Sparse Core Ops, SparseCore 0:
  950.1 740.1 all-reduce.103
where the time goes:
time: 1710 us; the launch traced here: 1700 us
  blocking collectives  460 us (27%)
  other arithmetic  428 us (25%)
  waiting for transfers between devices  355 us (21%)
  local copies, waits for them, and re-layouts  207 us (12%)
  starting transfers between devices  110 us (6%)
  matrix products  106 us (6%)
  loops' own time  18.3 us (1%)
    psum x1, blocking collectives, body(): summed = lax.psum(totals, 'dp')  460 us
    psum x1, waiting for transfers between devices, body(): summed = lax.psum(totals, 'dp')  276 us
    another operation x107, other arithmetic  112 us
    ppermute x22, starting transfers between devices, shifted_2(): return lax.ppermute(value, axis, pairs)  110 us
    scatter-add x88, local copies, waits for them, and re-layouts, backward_tick(): totals = tuple((t.at[loop_no].add(g) for t, g in zip(totals, grads)))  97.6 us
    ppermute x22, waiting for transfers between devices, shifted_2(): return lax.ppermute(value, axis, pairs)  79.2 us
    scatter-add x22, other arithmetic, backward_tick(): totals = tuple((t.at[loop_no].add(g) for t, g in zip(totals, grads)))  79 us
    dot_general x32, matrix products, block_apply(): jnp.dot(active, down_weight, preferred_element_type=jnp.float32) + down_bias  64.3 us
  transfers between devices with their start and end apart: 23, of which 12 were waited for; matrix products, arithmetic and copies ran while one was open for 17% of the time, Pallas kernels for 0%

commit v1 on v0

v1 whole, which is shorter than its diff:
```python
import functools
import jax
import jax.numpy as jnp
from jax import lax
from jax.experimental import pallas as pl
from jax.experimental.pallas import tpu as pltpu
from jax.sharding import PartitionSpec as P

C, HID, SIDE, NB = 320, 1280, 16, 8
CP = 384
CELLS = SIDE * SIDE
ROWS = 6656
BF, F32 = jnp.bfloat16, jnp.float32
K0, K1 = 0.7978845608028654, 0.044715
T_LANES = (((1,), (1,)), ((), ()))
T_ROWS = (((0,), (0,)), ((), ()))


def dot(a, b, dims=(((1,), (0,)), ((), ()))):
    return lax.dot_general(a, b, dims, preferred_element_type=F32)


def lane_tile(t):
    return pl.ds(pl.multiple_of(t * 128, 128), 128)


def conv_forward(pad_ref, small_ref, b, out_ref):
    def tile(t, _):
        lanes = lane_tile(t)
        for half in range(2):
            bias = jnp.broadcast_to(small_ref[b, 49:50, lanes], (8, 128))
            acc = [bias] * SIDE
            for dj in range(7):
                taps = [jnp.broadcast_to(small_ref[b, pl.ds(dr * 7 + dj, 1), lanes], (8, 128)) for dr in range(7)]
                for r in range(SIDE):
                    x = pad_ref[r, pl.ds(8 * half + 5 + dj, 8), lanes]
                    for dr in range(7):
                        i = r - dr + 3
                        if 0 <= i < SIDE:
                            acc[i] = acc[i] + x * taps[dr]
            for i in range(SIDE):
                out_ref[i, pl.ds(8 * half, 8), lanes] = acc[i]
        return 0

    lax.fori_loop(0, 3, tile, 0)


def conv_backward(gpad_ref, x_ref, small_ref, b, dx_ref, dk_ref):
    def tile(t, _):
        lanes = lane_tile(t)
        for half in range(2):
            xs = [x_ref[i, pl.ds(8 * half, 8), lanes] for i in range(SIDE)]
            acc = [jnp.zeros((8, 128), F32)] * SIDE
            for dj in range(7):
                taps = [jnp.broadcast_to(small_ref[b, pl.ds(dr * 7 + dj, 1), lanes], (8, 128)) for dr in range(7)]
                dks = [None] * 7
                for r in range(SIDE):
                    g = gpad_ref[r, pl.ds(8 * half + 11 - dj, 8), lanes]
                    for dr in range(7):
                        i = r + dr - 3
                        if 0 <= i < SIDE:
                            acc[i] = acc[i] + g * taps[dr]
                            p = g * xs[i]
                            dks[dr] = p if dks[dr] is None else dks[dr] + p
                for dr in range(7):
                    if half == 0:
                        dk_ref[dr * 7 + dj, :, lanes] = dks[dr]
                    else:
                        dk_ref[dr * 7 + dj, :, lanes] += dks[dr]
            for i in range(SIDE):
                dx_ref[i, pl.ds(8 * half, 8), lanes] = acc[i]
        return 0

    lax.fori_loop(0, 3, tile, 0)


def small_row(small_ref, b, row):
    return small_ref[b, row : row + 1, 0:C]


def up_bias_chunk(small_ref, b, n):
    parts = []
    for t in (2 * n, 2 * n + 1):
        parts.append(small_ref[b, 54 + t // 3 : 55 + t // 3, (t % 3) * 128 : (t % 3 + 1) * 128])
    return jnp.concatenate(parts, axis=1)


def window_of(h):
    cell = lax.broadcasted_iota(jnp.int32, (CELLS, 1), 0)
    return ((cell // SIDE < h) & (cell % SIDE < h)).astype(F32)


def block_forward(b, h, w_ref, small_ref, v_ref, pad_ref, mix_ref, act_ref, slope_ref, xhat_ref, inv_ref, proj_ref):
    v = v_ref[b].astype(F32)
    pad_ref[:, 8:24, 0:C] = v.reshape(SIDE, SIDE, C)
    conv_forward(pad_ref, small_ref, b, mix_ref)
    mixed = mix_ref[:, :, 0:C].reshape(CELLS, C)
    center = jnp.sum(mixed, axis=1, keepdims=True) * (1.0 / C)
    mixed = mixed - center
    inv = lax.rsqrt(jnp.sum(mixed * mixed, axis=1, keepdims=True) * (1.0 / C) + 1e-6)
    xhat = mixed * inv
    xhat_ref[b] = xhat
    inv_ref[b] = inv
    normed = (xhat * small_row(small_ref, b, 50) + small_row(small_ref, b, 51)).astype(BF)
    proj = jnp.broadcast_to(small_row(small_ref, b, 52), (CELLS, C))
    for n in range(5):
        cols = slice(256 * n, 256 * n + 256)
        u = dot(normed, w_ref[b, 0:C, cols]) + up_bias_chunk(small_ref, b, n)
        uu = u * u
        t = jnp.tanh(u * (K0 + (K0 * K1) * uu))
        lift = 0.5 + 0.5 * t
        act = (u * lift).astype(BF)
        slope = lift + (u * (0.5 - 0.5 * t * t)) * (K0 + (3 * K0 * K1) * uu)
        act_ref[b, :, cols] = act
        slope_ref[b, :, cols] = slope.astype(BF)
        proj = proj + dot(act, w_ref[b, C : 2 * C, cols], T_LANES)
    proj_ref[b] = proj.astype(BF)
    out = (v + small_row(small_ref, b, 53) * proj) * window_of(h)
    return out.astype(BF)


def block_backward(b, h, g, w_ref, small_ref, v_ref, pad_ref, mix_ref, x_ref, act_ref, slope_ref, xhat_ref, inv_ref, proj_ref, dk_ref, sg_ref, out_ref):
    g = g * window_of(h)
    sg_ref[53:54, 0:C] = jnp.sum(g * proj_ref[b].astype(F32), axis=0, keepdims=True)
    dproj = g * small_row(small_ref, b, 53)
    sg_ref[52:53, 0:C] = jnp.sum(dproj, axis=0, keepdims=True)
    dproj = dproj.astype(BF)
    xhat = xhat_ref[b]
    gain = small_row(small_ref, b, 50)
    normed = (xhat * gain + small_row(small_ref, b, 51)).astype(BF)
    dnormed = None
    for n in range(5):
        cols = slice(256 * n, 256 * n + 256)
        dact = dot(dproj, w_ref[b, C : 2 * C, cols])
        dhid = dact * slope_ref[b, :, cols].astype(F32)
        bias = jnp.sum(dhid, axis=0, keepdims=True)
        dhid = dhid.astype(BF)
        part = dot(dhid, w_ref[b, 0:C, cols], T_LANES)
        dnormed = part if dnormed is None else dnormed + part
        dup = dot(normed, dhid, T_ROWS).astype(BF)
        ddown = dot(dproj, act_ref[b, :, cols], T_ROWS).astype(BF)
        for k in range(2):
            t = 2 * n + k
            lanes = slice(128 * k, 128 * k + 128)
            out_ref[b, 320 * t : 320 * t + 320, :] = dup[:, lanes]
            out_ref[b, 3200 + 320 * t : 3520 + 320 * t, :] = ddown[:, lanes]
            sg_ref[54 + t // 3 : 55 + t // 3, (t % 3) * 128 : (t % 3 + 1) * 128] = bias[:, lanes]
    sg_ref[50:51, 0:C] = jnp.sum(dnormed * xhat, axis=0, keepdims=True)
    sg_ref[51:52, 0:C] = jnp.sum(dnormed, axis=0, keepdims=True)
    dxhat = dnormed * gain
    m0 = jnp.sum(dxhat, axis=1, keepdims=True) * (1.0 / C)
    m1 = jnp.sum(dxhat * xhat, axis=1, keepdims=True) * (1.0 / C)
    dmixed = inv_ref[b] * (dxhat - m0 - xhat * m1)
    sg_ref[49:50, 0:C] = jnp.sum(dmixed, axis=0, keepdims=True)
    pad_ref[:, 8:24, 0:C] = dmixed.reshape(SIDE, SIDE, C)
    x_ref[:, :, 0:C] = v_ref[b].astype(F32).reshape(SIDE, SIDE, C)
    conv_backward(pad_ref, x_ref, small_ref, b, mix_ref, dk_ref)
    sg_ref[0:49, :] = jnp.sum(dk_ref[...], axis=1)
    for j in range(3):
        out_ref[b, 6400 + 64 * j : 6464 + 64 * j, :] = sg_ref[:, 128 * j : 128 * j + 128].astype(BF)
    return (g + mix_ref[:, :, 0:C].reshape(CELLS, C)).astype(BF).astype(F32)


def clear(ref):
    ref[...] = jnp.zeros(ref.shape, ref.dtype)


def compute_kernel(h_ref, image_ref, cot_ref, w_ref, small_ref, out_ref, v_ref, pad_ref, mix_ref, x_ref, act_ref, slope_ref, xhat_ref, inv_ref, proj_ref, dk_ref, sg_ref, g_ref):
    h = h_ref[0]
    clear(pad_ref)
    clear(x_ref)
    clear(sg_ref)
    v_ref[0] = (image_ref[...].astype(F32) * window_of(h)).astype(BF)

    def forward(b, _):
        v_ref[b + 1] = block_forward(b, h, w_ref, small_ref, v_ref, pad_ref, mix_ref, act_ref, slope_ref, xhat_ref, inv_ref, proj_ref)
        return 0

    lax.fori_loop(0, NB, forward, 0)
    g_ref[...] = cot_ref[...].astype(F32)

    def backward(i, _):
        b = NB - 1 - i
        out_ref[b, 6592:6656, :] = jnp.zeros((64, 128), BF)
        g_ref[...] = block_backward(b, h, g_ref[...], w_ref, small_ref, v_ref, pad_ref, mix_ref, x_ref, act_ref, slope_ref, xhat_ref, inv_ref, proj_ref, dk_ref, sg_ref, out_ref)
        return 0

    lax.fori_loop(0, NB, backward, 0)


def compute_scratch():
    return [
        pltpu.VMEM((NB + 1, CELLS, C), BF),
        pltpu.VMEM((SIDE, 32, CP), F32),
        pltpu.VMEM((SIDE, SIDE, CP), F32),
        pltpu.VMEM((SIDE, SIDE, CP), F32),
        pltpu.VMEM((NB, CELLS, HID), BF),
        pltpu.VMEM((NB, CELLS, HID), BF),
        pltpu.VMEM((NB, CELLS, C), F32),
        pltpu.VMEM((NB, CELLS, 1), F32),
        pltpu.VMEM((NB, CELLS, C), BF),
        pltpu.VMEM((49, 8, CP), F32),
        pltpu.VMEM((64, CP), F32),
        pltpu.VMEM((CELLS, C), F32),
    ]


def compute(h, image, cot, weights, small):
    vm = pl.BlockSpec(memory_space=pltpu.VMEM)
    return pl.pallas_call(
        compute_kernel,
        out_shape=jax.ShapeDtypeStruct((NB, ROWS, 128), BF),
        in_specs=[pl.BlockSpec(memory_space=pltpu.SMEM), vm, vm, vm, vm],
        out_specs=vm,
        scratch_shapes=compute_scratch(),
        compiler_params=pltpu.CompilerParams(vmem_limit_bytes=60 * 2**20),
        cost_estimate=pl.CostEstimate(flops=12 * 10**9, bytes_accessed=30 * 10**6, transcendentals=3 * 10**6),
    )(h, image, cot, weights, small)


def pack_small(dw_kernel, dw_bias, gain, nbias, up_bias, down_bias, scale):
    n = dw_kernel.shape[0]
    rows = jnp.concatenate([dw_kernel.reshape(n, 49, C), dw_bias[:, None], gain[:, None], nbias[:, None], down_bias[:, None], scale[:, None]], axis=1)
    rows = jnp.pad(rows, ((0, 0), (0, 0), (0, CP - C)))
    up = jnp.pad(up_bias, ((0, 0), (0, 4 * CP - HID))).reshape(n, 4, CP)
    return jnp.concatenate([rows, up, jnp.zeros((n, 6, CP), F32)], axis=1)


HALF, QUART, PIECE = ROWS // 2, ROWS // 8, ROWS // 32
MESH = pl.DeviceIdType.MESH


class Place:
    def __init__(self):
        s, d = lax.axis_index("section"), lax.axis_index("dp")
        self.s, self.d = s, d
        self.core = d % 2
        self.z = (d // 32) * 4 + s
        self.step1 = 2 + 6 * self.core
        self.step2 = 10 - self.step1
        self.f1 = (d // self.step1) % 4
        self.f2 = (d // self.step2) % 4
        self.half = pl.multiple_of(self.core * HALF, HALF)

    def sibling(self):
        return (self.s, self.d + 1 - 2 * self.core)

    def first(self, k):
        q = (self.f1 + k) % 4
        return q, (self.s, self.d + (q - self.f1) * self.step1)

    def second(self, k):
        q = (self.f2 + k) % 4
        return q, (self.s, self.d + (q - self.f2) * self.step2)

    def up_z(self, k):
        z = (self.z + k) % 8
        return (z % 4, (z // 4) * 32 + self.d % 32)


def greet(devices):
    barrier = pltpu.get_barrier_semaphore()
    for device in devices:
        pl.semaphore_signal(barrier, inc=1, device_id=device, device_id_type=MESH)
    pl.semaphore_wait(barrier, len(devices))


def remote(src, dst, send, recv, device):
    return pltpu.make_async_remote_copy(src_ref=src, dst_ref=dst, send_sem=send, recv_sem=recv, device_id=device, device_id_type=MESH)


def add_into(dst_ref, b, base, count, src_refs):
    def step(i, _):
        rows = pl.ds(pl.multiple_of(base + i * PIECE, 16), PIECE)
        own = pl.ds(pl.multiple_of(i * PIECE, 16), PIECE)
        total = dst_ref[b, rows, :].astype(F32)
        for src in src_refs:
            total = total + src[own, :].astype(F32)
        dst_ref[b, rows, :] = total.astype(BF)
        return 0

    lax.fori_loop(0, count, step, 0)


class Reduce:
    def __init__(self, at, g_ref, fin_ref, cr, xr, yr, zr, sems):
        self.at, self.g, self.fin = at, g_ref, fin_ref
        self.cr, self.xr, self.yr, self.zr = cr, xr, yr, zr
        self.sems = sems

    def core_copy(self, b):
        at, (cs, crs) = self.at, self.sems[0]
        other = pl.multiple_of((1 - at.core) * HALF, HALF)
        return remote(self.g.at[b, pl.ds(other, HALF)], self.cr.at[b], cs.at[b], crs.at[b], at.sibling())

    def first_copy(self, b, k):
        at, (xs, xrs) = self.at, self.sems[1]
        q, device = at.first(k)
        rows = pl.ds(pl.multiple_of(at.half + q * QUART, 16), QUART)
        return remote(self.g.at[b, rows], self.xr.at[b, k - 1], xs.at[b, k - 1], xrs.at[b, k - 1], device)

    def second_copy(self, b, k):
        at, (ys, yrs) = self.at, self.sems[2]
        q, device = at.second(k)
        rows = pl.ds(pl.multiple_of(at.half + at.f1 * QUART + q * PIECE, 16), PIECE)
        return remote(self.g.at[b, rows], self.yr.at[b, k - 1], ys.at[b, k - 1], yrs.at[b, k - 1], device)

    def piece(self):
        at = self.at
        return pl.multiple_of(at.half + at.f1 * QUART + at.f2 * PIECE, 16)

    def z_copy(self, b, hi, source):
        at, (zs, zrs) = self.at, self.sems[3]
        device = (b % 4, hi * 32 + at.d % 32)
        return remote(self.g.at[b, pl.ds(self.piece(), PIECE)], self.zr.at[b // 4, source], zs.at[b, hi], zrs.at[b // 4, source], device)

    def back_second(self, l, k):
        at, (s, r) = self.at, self.sems[4]
        _, device = at.second(k)
        rows = pl.ds(self.piece(), PIECE)
        return remote(self.fin.at[l, rows], self.fin.at[l, rows], s.at[l, k - 1], r.at[l, k - 1], device)

    def back_second_in(self, l, k):
        at, (s, r) = self.at, self.sems[4]
        q, device = at.second(4 - k)
        rows = pl.ds(pl.multiple_of(at.half + at.f1 * QUART + q * PIECE, 16), PIECE)
        return remote(self.fin.at[l, rows], self.fin.at[l, rows], s.at[l, k - 1], r.at[l, k - 1], device)

    def back_first(self, l, k):
        at, (s, r) = self.at, self.sems[5]
        _, device = at.first(k)
        rows = pl.ds(pl.multiple_of(at.half + at.f1 * QUART, 16), QUART)
        return remote(self.fin.at[l, rows], self.fin.at[l, rows], s.at[l, k - 1], r.at[l, k - 1], device)

    def back_first_in(self, l, k):
        at, (s, r) = self.at, self.sems[5]
        q, device = at.first(4 - k)
        rows = pl.ds(pl.multiple_of(at.half + q * QUART, 16), QUART)
        return remote(self.fin.at[l, rows], self.fin.at[l, rows], s.at[l, k - 1], r.at[l, k - 1], device)

    def back_core(self, l, core):
        at, (s, r) = self.at, self.sems[6]
        rows = pl.ds(pl.multiple_of(core * HALF, HALF), HALF)
        return remote(self.fin.at[l, rows], self.fin.at[l, rows], s.at[l], r.at[l], at.sibling())

    def stage0(self, b):
        self.core_copy(b).start()

    def stage1(self, b):
        self.core_copy(b).wait()
        add_into(self.g, b, self.at.half, 16, [self.cr.at[b]])
        for k in (2, 1, 3):
            self.first_copy(b, k).start()

    def stage2(self, b):
        for k in (1, 2, 3):
            self.first_copy(b, k).wait()
        add_into(self.g, b, self.at.half + self.at.f1 * QUART, 4, [self.xr.at[b, k] for k in range(3)])
        for k in (2, 1, 3):
            self.second_copy(b, k).start()

    def stage3(self, b):
        at = self.at
        for k in (1, 2, 3):
            self.second_copy(b, k).wait()
        add_into(self.g, b, self.piece(), 1, [self.yr.at[b, k] for k in range(3)])
        for hi in range(2):
            @pl.when(at.z != hi * 4 + b % 4)
            def _():
                self.z_copy(b, hi, at.z).start()

    def stage4(self, b):
        at = self.at
        for hi in range(2):
            @pl.when(at.z != hi * 4 + b % 4)
            def _():
                self.z_copy(b, hi, at.z).wait_send()

        @pl.when(at.s == b % 4)
        def _():
            l = b // 4
            for k in range(1, 8):
                self.z_copy(b, 0, (at.z + k) % 8).wait_recv()
            rows = pl.ds(self.piece(), PIECE)
            self.zr[l, at.z] = self.g[b, rows, :]
            total = self.zr[l, 0].astype(F32)
            for z in range(1, 8):
                total = total + self.zr[l, z].astype(F32)
            self.fin[l, rows, :] = total.astype(BF)
            for k in (2, 1, 3):
                self.back_second(l, k).start()

    def stage5(self, b):
        at = self.at

        @pl.when(at.s == b % 4)
        def _():
            l = b // 4
            for k in (1, 2, 3):
                self.back_second(l, k).wait_send()
                self.back_second_in(l, k).wait_recv()
            for k in (2, 1, 3):
                self.back_first(l, k).start()

    def stage6(self, b):
        at = self.at

        @pl.when(at.s == b % 4)
        def _():
            l = b // 4
            for k in (1, 2, 3):
                self.back_first(l, k).wait_send()
                self.back_first_in(l, k).wait_recv()
            self.back_core(l, at.core).start()

    def stage7(self, b):
        at = self.at

        @pl.when(at.s == b % 4)
        def _():
            l = b // 4
            self.back_core(l, at.core).wait_send()
            self.back_core(l, 1 - at.core).wait_recv()

    def stages(self):
        return [self.stage0, self.stage1, self.stage2, self.stage3, self.stage4, self.stage5, self.stage6, self.stage7]


def reduce_partners(at):
    return [at.sibling()] + [at.first(k)[1] for k in (1, 2, 3)] + [at.second(k)[1] for k in (1, 2, 3)] + [at.up_z(k) for k in range(1, 8)]


def pair(*shape):
    return [pltpu.SemaphoreType.DMA(shape), pltpu.SemaphoreType.DMA(shape)]


def reduce_scratch():
    buffers = [
        pltpu.VMEM((NB, HALF, 128), BF),
        pltpu.VMEM((NB, 3, QUART, 128), BF),
        pltpu.VMEM((NB, 3, PIECE, 128), BF),
        pltpu.VMEM((2, 8, PIECE, 128), BF),
    ]
    sems = pair(NB) + pair(NB, 3) + pair(NB, 3)
    sems += [pltpu.SemaphoreType.DMA((NB, 2)), pltpu.SemaphoreType.DMA((2, 8))]
    sems += pair(2, 3) + pair(2, 3) + pair(2)
    return buffers + sems


def make_reduce(at, g_ref, fin_ref, refs):
    sems = [tuple(refs[4 + 2 * i : 6 + 2 * i]) for i in range(7)]
    return Reduce(at, g_ref, fin_ref, *refs[:4], sems)


def reduce_kernel(g_in, fin_ref, g_ref, copy_sem, *refs):
    at = Place()
    red = make_reduce(at, g_ref, fin_ref, refs)
    load = pltpu.make_async_copy(g_in, g_ref, copy_sem)
    load.start()
    greet(reduce_partners(at))
    load.wait()
    stages = red.stages()

    def tick(t, _):
        for n, stage in enumerate(stages):
            b = NB - 1 - (t - n)

            @pl.when((b >= 0) & (b < NB))
            def _():
                stage(b)
        return 0

    lax.fori_loop(0, NB + len(stages) - 1, tick, 0)


def reduce_grads(g):
    return pl.pallas_call(
        reduce_kernel,
        out_shape=jax.ShapeDtypeStruct((2, ROWS, 128), BF),
        in_specs=[pl.BlockSpec(memory_space=pl.ANY)],
        out_specs=pl.BlockSpec(memory_space=pltpu.VMEM),
        scratch_shapes=[pltpu.VMEM((NB, ROWS, 128), BF), pltpu.SemaphoreType.DMA] + reduce_scratch(),
        compiler_params=pltpu.CompilerParams(collective_id=1, has_side_effects=True, vmem_limit_bytes=60 * 2**20),
        cost_estimate=pl.CostEstimate(flops=10**7, bytes_accessed=30 * 10**6, transcendentals=0),
    )(g)


class Gather:
    def __init__(self, at, w_ref, small_ref, sems):
        self.at, self.w, self.small = at, w_ref, small_ref
        self.wz, self.sz, self.wc, self.sc = sems

    def rows(self, core, n):
        return pl.ds(pl.multiple_of(core * n, n), n)

    def copies(self, l, section, kind, device):
        at, b = self.at, l * 4 + section % 4
        w = self.w.at[b, self.rows(at.core, C)]
        small = self.small.at[b, self.rows(at.core, 32)]
        return [
            remote(w, w, self.wz[0].at[l, kind], self.wz[1].at[l, kind], device),
            remote(small, small, self.sz[0].at[l, kind], self.sz[1].at[l, kind], device),
        ]

    def across(self, l, section, kind, core):
        at, b = self.at, l * 4 + section % 4
        w = self.w.at[b, self.rows(core, C)]
        small = self.small.at[b, self.rows(core, 32)]
        return [
            remote(w, w, self.wc[0].at[l, kind], self.wc[1].at[l, kind], at.sibling()),
            remote(small, small, self.sc[0].at[l, kind], self.sc[1].at[l, kind], at.sibling()),
        ]

    def begin(self, l):
        at = self.at
        for kind, k in ((0, 1), (1, -1)):
            for c in self.copies(l, at.s, kind, at.up_z(k)):
                c.start()

    def pass_on(self, l):
        at = self.at
        for kind, k in ((0, -1), (1, 1)):
            for c in self.copies(l, at.s + 4 + k, kind, at.up_z(k)):
                c.wait_recv()
            onward = at.core == 1 - kind

            @pl.when(onward)
            def _():
                for c in self.copies(l, at.s + 4 + k, 2, at.up_z(-k)):
                    c.start()
            for c in self.across(l, at.s + 4 + k, kind, at.core):
                c.start()

    def finish(self, l):
        at = self.at
        far = at.up_z(1)
        for c in self.copies(l, at.s + 2, 2, far):
            c.wait_recv()
        for c in self.across(l, at.s + 2, 2, at.core):
            c.start()
        for kind, k in ((0, -1), (1, 1), (2, 2)):
            for c in self.across(l, at.s + 4 + k, kind, 1 - at.core):
                c.wait_recv()

    def drain(self, l):
        at = self.at
        for kind in range(3):
            for c in self.copies(l, at.s, kind, at.up_z(1)):
                c.wait_send()
            for c in self.across(l, at.s, kind, at.core):
                c.wait_send()


def gather_partners(at):
    return [at.sibling(), at.up_z(1), at.up_z(-1)]


def gather_scratch():
    return pair(2, 3) + pair(2, 3) + pair(2, 3) + pair(2, 3)


def make_gather(at, w_ref, small_ref, sems):
    return Gather(at, w_ref, small_ref, [tuple(sems[2 * i : 2 * i + 2]) for i in range(4)])


def gather_kernel(w_in, small_in, w_ref, small_ref, own_sem, *sems):
    at = Place()
    own = []
    for l in range(2):
        own.append(pltpu.make_async_copy(w_in.at[l], w_ref.at[l * 4 + at.s], own_sem.at[l, 0]))
        own.append(pltpu.make_async_copy(small_in.at[l], small_ref.at[l * 4 + at.s], own_sem.at[l, 1]))
    for c in own:
        c.start()
    greet(gather_partners(at))
    for c in own:
        c.wait()
    gather = make_gather(at, w_ref, small_ref, sems)
    for l in range(2):
        gather.begin(l)
    for l in range(2):
        gather.pass_on(l)
        gather.finish(l)
    for l in range(2):
        gather.drain(l)


def gather_weights(w, small):
    anyw = pl.BlockSpec(memory_space=pl.ANY)
    vm = pl.BlockSpec(memory_space=pltpu.VMEM)
    return pl.pallas_call(
        gather_kernel,
        out_shape=(jax.ShapeDtypeStruct((NB, 2 * C, HID), BF), jax.ShapeDtypeStruct((NB, 64, CP), F32)),
        in_specs=[anyw, anyw],
        out_specs=(vm, vm),
        scratch_shapes=[pltpu.SemaphoreType.DMA((2, 2))] + gather_scratch(),
        compiler_params=pltpu.CompilerParams(collective_id=0, has_side_effects=True, vmem_limit_bytes=60 * 2**20),
        cost_estimate=pl.CostEstimate(flops=10**6, bytes_accessed=30 * 10**6, transcendentals=0),
    )(w, small)


def unpack(fin):
    up = fin[:, :3200].reshape(2, 10, C, 128).transpose(0, 2, 1, 3).reshape(2, C, HID)
    down = fin[:, 3200:6400].reshape(2, 10, C, 128).transpose(0, 1, 3, 2).reshape(2, HID, C)
    small = fin[:, 6400:6592].astype(F32).reshape(2, 3, 64, 128).transpose(0, 2, 1, 3).reshape(2, 64, CP)
    up_bias = small[:, 54:58].reshape(2, 4 * CP)[:, :HID]
    row = lambda i: small[:, i, :C]
    parts = (small[:, :49, :C].reshape(2, 7, 7, C), row(49), row(50), row(51), up, up_bias, down, row(52), row(53))
    return tuple(p[:, None] for p in parts)


def body(images, cotangent, heights, dw_kernel, dw_bias, norm_gain, norm_bias, up_weight, up_bias, down_weight, down_bias, layer_scale):
    s = lax.axis_index("section")
    pick = lambda a: lax.dynamic_index_in_dim(a[:, 0], s, 0, keepdims=False).reshape(CELLS, C)
    w = jnp.concatenate([up_weight[:, 0], down_weight[:, 0].swapaxes(1, 2)], axis=1)
    small = pack_small(*(a[:, 0] for a in (dw_kernel, dw_bias, norm_gain, norm_bias, up_bias, down_bias, layer_scale)))
    height = lax.dynamic_slice_in_dim(heights, s, 1)
    w_all, small_all = gather_weights(w, small)
    grads = compute(height, pick(images), pick(cotangent), w_all, small_all)
    return unpack(reduce_grads(grads))


def solution(mesh):
    three, two = P(None, "section", None, None), P(None, "section", None)
    five = P(None, "section", None, None, None)
    image = P(None, "dp", None, None, None)
    weights = (five, two, two, two, three, two, three, two, two)
    return jax.shard_map(body, mesh=mesh, in_specs=(image, image, P()) + weights, out_specs=weights, check_vma=False)
```

time: 1710 us -> 312 us (0.18)
  blocking collectives: 460 us -> 0 us
  other arithmetic: 428 us -> 4.07 us
  waiting for transfers between devices: 355 us -> 0 us
  Pallas kernels: 0 us -> 285 us
  local copies, waits for them, and re-layouts: 207 us -> 22 us
  starting transfers between devices: 110 us -> 0 us
  matrix products: 106 us -> 0 us
  loops' own time: 18.3 us -> 0 us
    psum x1 -> x0, blocking collectives: 460 us -> none  [body(): summed = lax.psum(totals, 'dp')]
    pallas_call x0 -> x3, Pallas kernels: none -> 285 us  [the longest x1 114 us: compute(): pl.pallas_call(compute_kernel, out_shape=jax.ShapeDtypeStruct((NB, ROWS,...]
    psum x1 -> x0, waiting for transfers between devices: 276 us -> none  [body(): summed = lax.psum(totals, 'dp')]
    another operation x107 -> x0, other arithmetic: 112 us -> none
    ppermute x22 -> x0, starting transfers between devices: 110 us -> none  [shifted_2(): return lax.ppermute(value, axis, pairs)]
    reduce_sum x80 -> x0, other arithmetic: 107 us -> none  [the longest x16 59.6 us: block_apply(): center = jnp.mean(mixed, axis=-1, keepdims=True)]
    dot_general x56 -> x0, matrix products: 106 us -> none  [the longest x32 64.3 us: block_apply(): jnp.dot(active, down_weight, preferred_element_type=jnp.float32) + down_bias]
    scatter-add x88 -> x0, local copies, waits for them, and re-layouts: 97.6 us -> none  [backward_tick(): totals = tuple((t.at[loop_no].add(g) for t, g in zip(totals, grads)))]
  transfers between devices with their start and end apart: 23 -> 0, of which waited for: 12 -> 0; matrix products, arithmetic and copies ran while one was open for 17% -> 0% of each run, Pallas kernels for 0% -> 0%
where the time goes in v1:
time: 312 us
  Pallas kernels  285 us (91%)
  local copies, waits for them, and re-layouts  22 us (7%)
  other arithmetic  4.07 us (1%)
    pallas_call x1, Pallas kernels, compute(): pl.pallas_call(compute_kernel, out_shape=jax.ShapeDtypeStruct((NB, ROWS,...  114 us
    pallas_call x1, Pallas kernels, reduce_grads(): pl.pallas_call(reduce_kernel, out_shape=jax.ShapeDtypeStruct((2, ROWS, 12...  94.1 us
    pallas_call x1, Pallas kernels, gather_weights(): pl.pallas_call(gather_kernel, out_shape=(jax.ShapeDtypeStruct((NB, 2 * C,...  76.9 us
    unnamed x9, local copies, waits for them, and re-layouts  7.12 us

profile of v1, /device:TPU:1, one launch (start us, length us, event | category | flops | bytes accessed | tf_op | source)
XLA Modules:
  0.0 311.8 jit_solution(325989530612706763)
XLA Ops:
  0.6 0.0 copy-start
  0.7 1.4 dynamic_slice.10.h_ref
  2.0 0.1 pad.12.clone
  2.1 0.7 copy.46
  2.8 1.0 copy.32
  3.9 0.8 concatenate.10
  4.7 0.8 fusion.small_in
  5.4 1.8 constant_dynamic-slice_fusion
  7.2 3.3 %pad_maximum_fusion.w_in = bf16[2,640,1280]{2,1,0:T(8,128)(2,1)} fusion(bf16[2,320,1280]{2,1,0:T(8,128)(2,1)S(1)} %bitcast.32, bf16[2,320,1280]{2,1,0:T(8,128)(2,1)} %bitcast.33), kind=kLoop, calls=%fused_computation | loop fusion | flops 6553600 | bytes 6553600 | tf_op jit(solution)/shard_map/concatenate | solution.py:614
  10.5 76.9 %shard_map.187 = (bf16[8,640,1280]{2,1,0:T(8,128)(2,1)}, f32[8,64,384]{2,1,0:T(8,128)}) custom-call(bf16[2,640,1280]{2,1,0:T(8,128)(2,1)} %pad_maximum_fusion.w_in, f32[2,64,384]{2,1,0:T(8,128)} %fusion.small_in), custom_call_target="tpu_custom_call" | custom-call | flops 1000000 | bytes 30000000 | tf_op jit(solution)/shard_map/pallas_call | solution.py:590
  87.5 114.0 %shard_map.188.g_in = bf16[8,6656,128]{2,1,0:T(8,128)(2,1)} custom-call(s32[1]{0:T(128)} %dynamic_slice.10.h_ref, bf16[256,320]{1,0:T(8,128)(2,1)} %bitcast.38, bf16[256,320]{1,0:T(8,128)(2,1)} %bitcast.37, bf16[8,640,1280]{2,1,0:T(8,128)(2,1)} %get-tuple-element.11.w_ref, f32[8,64,384]{2,1,0:T(8,128)} %get-tuple-element.12.small_ref), custom_call_target="tpu_custom_call" | custom-call | flops 12000000000 | bytes 30000000 | tf_op jit(solution)/shard_map/pallas_call | solution.py:210
  201.4 94.1 %shard_map.189 = bf16[2,6656,128]{2,1,0:T(8,128)(2,1)} custom-call(bf16[8,6656,128]{2,1,0:T(8,128)(2,1)} %shard_map.188.g_in), custom_call_target="tpu_custom_call" | custom-call | flops 10000000 | bytes 30000000 | tf_op jit(solution)/shard_map/pallas_call | solution.py:477
  295.6 0.0 slice-start
  295.6 3.9 %fusion.1 = (bf16[2,3200,128]{2,1,0:T(8,128)(2,1)}, bf16[2,3200,128]{2,1,0:T(8,128)(2,1)}) fusion(bf16[2,6656,128]{2,1,0:T(8,128)(2,1)} %shard_map.189), kind=kLoop, calls=%fused_computation.9 | loop fusion | bytes 6553600 | tf_op jit(solution)/shard_map/slice | solution.py:603
  299.4 0.1 copy.45
  299.5 0.1 reshape.62
  299.7 0.6 broadcast_in_dim.7
  300.3 0.6 fusion.2
  300.9 0.1 copy.35
  301.0 0.8 copy.38
  301.8 2.7 copy.36
  304.5 2.3 copy.39
  306.8 2.7 copy.37
  309.6 2.3 copy.40
  (10 shorter events, 0.1 us)
Async XLA Ops:
  0.6 6.6 %copy-start = (bf16[2,1,1280,320]{2,3,1,0:T(8,128)(2,1)S(1)}, bf16[2,1,1280,320]{2,3,1,0:T(8,128)(2,1)}, u32[]{:S(2)}) copy-start(bf16[2,1,1280,320]{2,3,1,0:T(8,128)(2,1)} %param.21) | copy-start | bytes 4915204
  295.6 3.9 %slice-start = ((bf16[2,6656,128]{2,1,0:T(8,128)(2,1)}), bf16[2,192,128]{2,1,0:T(8,128)(2,1)S(1)}, s32[]{:S(2)}) async-start(bf16[2,6656,128]{2,1,0:T(8,128)(2,1)} %shard_map.189), calls=%async_computation | async-start | bytes 196608 | tf_op jit(solution)/shard_map/slice | solution.py:604

commit v2 on v1

v2 whole, which is shorter than its diff:
```python
import jax
import jax.numpy as jnp
from jax import lax
from jax.experimental import pallas as pl
from jax.experimental.pallas import tpu as pltpu
from jax.sharding import PartitionSpec as P

C, HID, SIDE, NB = 320, 1280, 16, 8
CP = 384
CELLS = SIDE * SIDE
ROWS = 6656
BF, F32 = jnp.bfloat16, jnp.float32
K0, K1 = 0.7978845608028654, 0.044715
T_LANES = (((1,), (1,)), ((), ()))
T_ROWS = (((0,), (0,)), ((), ()))


def dot(a, b, dims=(((1,), (0,)), ((), ()))):
    return lax.dot_general(a, b, dims, preferred_element_type=F32)


def lane_tile(t):
    return pl.ds(pl.multiple_of(t * 128, 128), 128)


def shift_columns(pad_ref, shift_ref, first, step):
    for dj in range(7):
        at = first + step * dj
        shift_ref[dj] = pad_ref[:, at : at + SIDE, :]


def taps_of(small_ref, b, dj, lanes):
    return [jnp.broadcast_to(small_ref[b, dr * 7 + dj : dr * 7 + dj + 1, lanes], (8, 128)) for dr in range(7)]


def conv_forward(shift_ref, small_ref, b, out_ref):
    def tile(t, _):
        lanes = lane_tile(t)
        for half in range(2):
            cols = pl.ds(8 * half, 8)
            acc = [jnp.broadcast_to(small_ref[b, 49:50, lanes], (8, 128))] * SIDE
            for dj in range(7):
                taps = taps_of(small_ref, b, dj, lanes)
                for r in range(SIDE):
                    x = shift_ref[dj, r, cols, lanes]
                    for dr in range(7):
                        i = r - dr + 3
                        if 0 <= i < SIDE:
                            acc[i] = acc[i] + x * taps[dr]
            for i in range(SIDE):
                out_ref[i, cols, lanes] = acc[i]
        return 0

    lax.fori_loop(0, 3, tile, 0)


def conv_backward(shift_ref, x_ref, small_ref, b, dx_ref, dk_ref):
    def tile(t, _):
        lanes = lane_tile(t)
        for half in range(2):
            cols = pl.ds(8 * half, 8)
            xs = [x_ref[i, cols, lanes] for i in range(SIDE)]
            acc = [None] * SIDE
            for dj in range(7):
                taps = taps_of(small_ref, b, dj, lanes)
                dks = [None] * 7
                for r in range(SIDE):
                    g = shift_ref[dj, r, cols, lanes]
                    for dr in range(7):
                        i = r + dr - 3
                        if 0 <= i < SIDE:
                            p = g * taps[dr]
                            acc[i] = p if acc[i] is None else acc[i] + p
                            p = g * xs[i]
                            dks[dr] = p if dks[dr] is None else dks[dr] + p
                for dr in range(7):
                    if half == 0:
                        dk_ref[dr * 7 + dj, :, lanes] = dks[dr]
                    else:
                        dk_ref[dr * 7 + dj, :, lanes] += dks[dr]
            for i in range(SIDE):
                dx_ref[i, cols, lanes] = acc[i]
        return 0

    lax.fori_loop(0, 3, tile, 0)


def weight_chunk(w_ref, b, base, n):
    at = base + 640 * n
    return jnp.concatenate([w_ref[b, at : at + C, :], w_ref[b, at + C : at + 2 * C, :]], axis=1)


def small_row(small_ref, b, row):
    return small_ref[b, row : row + 1, 0:C]


def up_bias_chunk(small_ref, b, n):
    parts = []
    for t in (2 * n, 2 * n + 1):
        parts.append(small_ref[b, 54 + t // 3 : 55 + t // 3, (t % 3) * 128 : (t % 3 + 1) * 128])
    return jnp.concatenate(parts, axis=1)


def window_of(h):
    cell = lax.broadcasted_iota(jnp.int32, (CELLS, 1), 0)
    return ((cell // SIDE < h) & (cell % SIDE < h)).astype(F32)


def block_forward(b, h, w_ref, small_ref, v_ref, pad_ref, shift_ref, mix_ref, act_ref, slope_ref, xhat_ref, inv_ref, proj_ref):
    v = v_ref[b].astype(F32)
    pad_ref[:, 8:24, 0:C] = v.reshape(SIDE, SIDE, C)
    shift_columns(pad_ref, shift_ref, 5, 1)
    conv_forward(shift_ref, small_ref, b, mix_ref)
    mixed = mix_ref[:, :, 0:C].reshape(CELLS, C)
    center = jnp.sum(mixed, axis=1, keepdims=True) * (1.0 / C)
    mixed = mixed - center
    inv = lax.rsqrt(jnp.sum(mixed * mixed, axis=1, keepdims=True) * (1.0 / C) + 1e-6)
    xhat = mixed * inv
    xhat_ref[b] = xhat
    inv_ref[b] = inv
    normed = (xhat * small_row(small_ref, b, 50) + small_row(small_ref, b, 51)).astype(BF)
    proj = jnp.broadcast_to(small_row(small_ref, b, 52), (CELLS, C))
    for n in range(5):
        cols = slice(256 * n, 256 * n + 256)
        u = dot(normed, weight_chunk(w_ref, b, 0, n)) + up_bias_chunk(small_ref, b, n)
        uu = u * u
        t = jnp.tanh(u * (K0 + (K0 * K1) * uu))
        lift = 0.5 + 0.5 * t
        act = (u * lift).astype(BF)
        slope = lift + (u * (0.5 - 0.5 * t * t)) * (K0 + (3 * K0 * K1) * uu)
        act_ref[b, :, cols] = act
        slope_ref[b, :, cols] = slope.astype(BF)
        proj = proj + dot(act, weight_chunk(w_ref, b, 3200, n), T_LANES)
    proj_ref[b] = proj.astype(BF)
    out = (v + small_row(small_ref, b, 53) * proj) * window_of(h)
    return out.astype(BF)


def block_backward(b, h, g, w_ref, small_ref, v_ref, pad_ref, shift_ref, mix_ref, x_ref, act_ref, slope_ref, xhat_ref, inv_ref, proj_ref, dk_ref, sg_ref):
    g = g * window_of(h)
    sg_ref[53:54, 0:C] = jnp.sum(g * proj_ref[b].astype(F32), axis=0, keepdims=True)
    dproj = g * small_row(small_ref, b, 53)
    sg_ref[52:53, 0:C] = jnp.sum(dproj, axis=0, keepdims=True)
    dproj = dproj.astype(BF)
    xhat = xhat_ref[b]
    gain = small_row(small_ref, b, 50)
    normed = (xhat * gain + small_row(small_ref, b, 51)).astype(BF)
    dnormed = None
    for n in range(5):
        cols = slice(256 * n, 256 * n + 256)
        dact = dot(dproj, weight_chunk(w_ref, b, 3200, n))
        dhid = dact * slope_ref[b, :, cols].astype(F32)
        bias = jnp.sum(dhid, axis=0, keepdims=True)
        dhid = dhid.astype(BF)
        part = dot(dhid, weight_chunk(w_ref, b, 0, n), T_LANES)
        dnormed = part if dnormed is None else dnormed + part
        dup = dot(normed, dhid, T_ROWS).astype(BF)
        ddown = dot(dproj, act_ref[b, :, cols], T_ROWS).astype(BF)
        for k in range(2):
            t = 2 * n + k
            lanes = slice(128 * k, 128 * k + 128)
            w_ref[b, 320 * t : 320 * t + 320, :] = dup[:, lanes]
            w_ref[b, 3200 + 320 * t : 3520 + 320 * t, :] = ddown[:, lanes]
            sg_ref[54 + t // 3 : 55 + t // 3, (t % 3) * 128 : (t % 3 + 1) * 128] = bias[:, lanes]
    sg_ref[50:51, 0:C] = jnp.sum(dnormed * xhat, axis=0, keepdims=True)
    sg_ref[51:52, 0:C] = jnp.sum(dnormed, axis=0, keepdims=True)
    dxhat = dnormed * gain
    m0 = jnp.sum(dxhat, axis=1, keepdims=True) * (1.0 / C)
    m1 = jnp.sum(dxhat * xhat, axis=1, keepdims=True) * (1.0 / C)
    dmixed = inv_ref[b] * (dxhat - m0 - xhat * m1)
    sg_ref[49:50, 0:C] = jnp.sum(dmixed, axis=0, keepdims=True)
    pad_ref[:, 8:24, 0:C] = dmixed.reshape(SIDE, SIDE, C)
    x_ref[:, :, 0:C] = v_ref[b].astype(F32).reshape(SIDE, SIDE, C)
    shift_columns(pad_ref, shift_ref, 11, -1)
    conv_backward(shift_ref, x_ref, small_ref, b, mix_ref, dk_ref)
    sg_ref[0:49, :] = jnp.sum(dk_ref[...], axis=1)
    for j in range(3):
        w_ref[b, 6400 + 64 * j : 6464 + 64 * j, :] = sg_ref[:, 128 * j : 128 * j + 128].astype(BF)
    return (g + mix_ref[:, :, 0:C].reshape(CELLS, C)).astype(BF).astype(F32)


def clear(ref):
    ref[...] = jnp.zeros(ref.shape, ref.dtype)


def pack_small(dw_kernel, dw_bias, gain, nbias, up_bias, down_bias, scale):
    n = dw_kernel.shape[0]
    rows = jnp.concatenate([dw_kernel.reshape(n, 49, C), dw_bias[:, None], gain[:, None], nbias[:, None], down_bias[:, None], scale[:, None]], axis=1)
    rows = jnp.pad(rows, ((0, 0), (0, 0), (0, CP - C)))
    up = jnp.pad(up_bias, ((0, 0), (0, 4 * CP - HID))).reshape(n, 4, CP)
    return jnp.concatenate([rows, up, jnp.zeros((n, 6, CP), F32)], axis=1)


HALF, QUART, PIECE = ROWS // 2, ROWS // 8, ROWS // 32
MESH = pl.DeviceIdType.MESH


class Place:
    def __init__(self):
        s, d = lax.axis_index("section"), lax.axis_index("dp")
        self.s, self.d = s, d
        self.core = d % 2
        self.z = (d // 32) * 4 + s
        self.step1 = 2 + 6 * self.core
        self.step2 = 10 - self.step1
        self.f1 = (d // self.step1) % 4
        self.f2 = (d // self.step2) % 4
        self.half = pl.multiple_of(self.core * HALF, HALF)
        self.x, self.y = (d // 2) % 4, (d // 8) % 4
        self.color = (self.x + self.y) % 2

    def sibling(self):
        return (self.s, self.d + 1 - 2 * self.core)

    def first(self, k):
        q = (self.f1 + k) % 4
        return q, (self.s, self.d + (q - self.f1) * self.step1)

    def second(self, k):
        q = (self.f2 + k) % 4
        return q, (self.s, self.d + (q - self.f2) * self.step2)

    def beside(self, side):
        step, at = (2, self.x) if side < 2 else (8, self.y)
        k = 1 if side % 2 == 0 else 3
        return (self.s, self.d + ((at + k) % 4 - at) * step)

    def up_z(self, k):
        z = (self.z + k) % 8
        return (z % 4, (z // 4) * 32 + self.d % 32)


def greet(devices):
    barrier = pltpu.get_barrier_semaphore()
    for device in devices:
        pl.semaphore_signal(barrier, inc=1, device_id=device, device_id_type=MESH)
    pl.semaphore_wait(barrier, len(devices))


def remote(src, dst, send, recv, device):
    return pltpu.make_async_remote_copy(src_ref=src, dst_ref=dst, send_sem=send, recv_sem=recv, device_id=device, device_id_type=MESH)


def add_into(dst_ref, b, base, count, src_refs):
    def step(i, _):
        rows = pl.ds(pl.multiple_of(base + i * PIECE, 16), PIECE)
        own = pl.ds(pl.multiple_of(i * PIECE, 16), PIECE)
        total = dst_ref[b, rows, :].astype(F32)
        for src in src_refs:
            total = total + src[own, :].astype(F32)
        dst_ref[b, rows, :] = total.astype(BF)
        return 0

    lax.fori_loop(0, count, step, 0)


class Reduce:
    def __init__(self, at, g_ref, outs, fin_ref, cr, xr, yr, zr, sems):
        self.at, self.g, self.fin = at, g_ref, fin_ref
        self.up, self.down, self.small = outs
        self.cr, self.xr, self.yr, self.zr = cr, xr, yr, zr
        self.sems = sems

    def core_copy(self, b):
        at, (cs, crs) = self.at, self.sems[0]
        other = pl.multiple_of((1 - at.core) * HALF, HALF)
        return remote(self.g.at[b, pl.ds(other, HALF)], self.cr.at[b], cs.at[b], crs.at[b], at.sibling())

    def first_copy(self, b, k):
        at, (xs, xrs) = self.at, self.sems[1]
        q, device = at.first(k)
        rows = pl.ds(pl.multiple_of(at.half + q * QUART, 16), QUART)
        return remote(self.g.at[b, rows], self.xr.at[b, k - 1], xs.at[b, k - 1], xrs.at[b, k - 1], device)

    def second_copy(self, b, k):
        at, (ys, yrs) = self.at, self.sems[2]
        q, device = at.second(k)
        rows = pl.ds(pl.multiple_of(at.half + at.f1 * QUART + q * PIECE, 16), PIECE)
        return remote(self.g.at[b, rows], self.yr.at[b, k - 1], ys.at[b, k - 1], yrs.at[b, k - 1], device)

    def piece(self):
        at = self.at
        return pl.multiple_of(at.half + at.f1 * QUART + at.f2 * PIECE, 16)

    def z_copy(self, b, hi, source):
        at, (zs, zrs) = self.at, self.sems[3]
        device = (b % 4, hi * 32 + at.d % 32)
        return remote(self.g.at[b, pl.ds(self.piece(), PIECE)], self.zr.at[b // 4, source], zs.at[b, hi], zrs.at[b // 4, source], device)

    def back_second(self, l, k):
        at, (s, r) = self.at, self.sems[4]
        _, device = at.second(k)
        rows = pl.ds(self.piece(), PIECE)
        return remote(self.fin.at[l, rows], self.fin.at[l, rows], s.at[l, k - 1], r.at[l, k - 1], device)

    def back_second_in(self, l, k):
        at, (s, r) = self.at, self.sems[4]
        q, device = at.second(4 - k)
        rows = pl.ds(pl.multiple_of(at.half + at.f1 * QUART + q * PIECE, 16), PIECE)
        return remote(self.fin.at[l, rows], self.fin.at[l, rows], s.at[l, k - 1], r.at[l, k - 1], device)

    def back_first(self, l, k):
        at, (s, r) = self.at, self.sems[5]
        _, device = at.first(k)
        rows = pl.ds(pl.multiple_of(at.half + at.f1 * QUART, 16), QUART)
        return remote(self.fin.at[l, rows], self.fin.at[l, rows], s.at[l, k - 1], r.at[l, k - 1], device)

    def back_first_in(self, l, k):
        at, (s, r) = self.at, self.sems[5]
        q, device = at.first(4 - k)
        rows = pl.ds(pl.multiple_of(at.half + q * QUART, 16), QUART)
        return remote(self.fin.at[l, rows], self.fin.at[l, rows], s.at[l, k - 1], r.at[l, k - 1], device)

    def back_core(self, l, core):
        at, (s, r) = self.at, self.sems[6]
        rows = pl.ds(pl.multiple_of(core * HALF, HALF), HALF)
        return remote(self.fin.at[l, rows], self.fin.at[l, rows], s.at[l], r.at[l], at.sibling())

    def stage0(self, b):
        self.core_copy(b).start()

    def stage1(self, b):
        self.core_copy(b).wait()
        add_into(self.g, b, self.at.half, 16, [self.cr.at[b]])
        for k in (2, 1, 3):
            self.first_copy(b, k).start()

    def stage2(self, b):
        for k in (1, 2, 3):
            self.first_copy(b, k).wait()
        add_into(self.g, b, self.at.half + self.at.f1 * QUART, 4, [self.xr.at[b, k] for k in range(3)])
        for k in (2, 1, 3):
            self.second_copy(b, k).start()

    def stage3(self, b):
        at = self.at
        for k in (1, 2, 3):
            self.second_copy(b, k).wait()
        add_into(self.g, b, self.piece(), 1, [self.yr.at[b, k] for k in range(3)])
        for hi in range(2):
            @pl.when(at.z != hi * 4 + b % 4)
            def _():
                self.z_copy(b, hi, at.z).start()

    def stage4(self, b):
        at = self.at
        for hi in range(2):
            @pl.when(at.z != hi * 4 + b % 4)
            def _():
                self.z_copy(b, hi, at.z).wait_send()

        @pl.when(at.s == b % 4)
        def _():
            l = b // 4
            for k in range(1, 8):
                self.z_copy(b, 0, (at.z + k) % 8).wait_recv()
            rows = pl.ds(self.piece(), PIECE)
            self.zr[l, at.z] = self.g[b, rows, :]
            total = self.zr[l, 0].astype(F32)
            for z in range(1, 8):
                total = total + self.zr[l, z].astype(F32)
            self.fin[l, rows, :] = total.astype(BF)
            for k in (2, 1, 3):
                self.back_second(l, k).start()

    def stage5(self, b):
        at = self.at

        @pl.when(at.s == b % 4)
        def _():
            l = b // 4
            for k in (1, 2, 3):
                self.back_second(l, k).wait_send()
                self.back_second_in(l, k).wait_recv()
            for k in (2, 1, 3):
                self.back_first(l, k).start()

    def stage6(self, b):
        at = self.at

        @pl.when(at.s == b % 4)
        def _():
            l = b // 4
            for k in (1, 2, 3):
                self.back_first(l, k).wait_send()
                self.back_first_in(l, k).wait_recv()
            self.back_core(l, at.core).start()

    def stage7(self, b):
        at = self.at

        @pl.when(at.s == b % 4)
        def _():
            l = b // 4
            self.back_core(l, at.core).wait_send()
            self.back_core(l, 1 - at.core).wait_recv()
            for t in range(10):
                lanes = slice(128 * t, 128 * t + 128)
                self.up[l, :, lanes] = self.fin[l, C * t : C * t + C, :]
                self.down[l, :, lanes] = self.fin[l, 3200 + C * t : 3200 + C * t + C, :]
            for t in range(3):
                self.small[l, :, 128 * t : 128 * t + 128] = self.fin[l, 6400 + 64 * t : 6464 + 64 * t, :].astype(F32)

    def stages(self):
        return [self.stage0, self.stage1, self.stage2, self.stage3, self.stage4, self.stage5, self.stage6, self.stage7]


def reduce_partners(at):
    return [at.sibling()] + [at.first(k)[1] for k in (1, 2, 3)] + [at.second(k)[1] for k in (1, 2, 3)] + [at.up_z(k) for k in range(1, 8)]


def pair(*shape):
    return [pltpu.SemaphoreType.DMA(shape), pltpu.SemaphoreType.DMA(shape)]


def reduce_scratch():
    buffers = [
        pltpu.VMEM((2, ROWS, 128), BF),
        pltpu.VMEM((NB, HALF, 128), BF),
        pltpu.VMEM((NB, 3, QUART, 128), BF),
        pltpu.VMEM((NB, 3, PIECE, 128), BF),
        pltpu.VMEM((2, 8, PIECE, 128), BF),
    ]
    sems = pair(NB) + pair(NB, 3) + pair(NB, 3)
    sems += [pltpu.SemaphoreType.DMA((NB, 2)), pltpu.SemaphoreType.DMA((2, 8))]
    sems += pair(2, 3) + pair(2, 3) + pair(2)
    return buffers + sems


def make_reduce(at, g_ref, outs, refs):
    sems = [tuple(refs[5 + 2 * i : 7 + 2 * i]) for i in range(7)]
    return Reduce(at, g_ref, outs, *refs[:5], sems)


WHALF, SHARE, PART = 3200, 1600, 400


class Gather:
    def __init__(self, at, w_ref, small_ref, sems):
        self.at, self.w, self.small_ref = at, w_ref, small_ref
        self.zs, self.ps, self.cs, self.small_zs, self.small_cs = sems

    def block(self, l, kind):
        return l * 4 + (self.at.s + (3, 1, 2)[kind]) % 4

    def share(self, core, color):
        return pl.multiple_of(core * WHALF + color * SHARE, 16)

    def along_z(self, l, b, kind, device):
        at = self.at
        w = self.w.at[b, pl.ds(self.share(at.core, at.color), SHARE)]
        small = self.small_ref.at[b, pl.ds(pl.multiple_of(at.core * 32, 32), 32)]
        return [
            remote(w, w, self.zs[0].at[l, kind], self.zs[1].at[l, kind], device),
            remote(small, small, self.small_zs[0].at[l, kind], self.small_zs[1].at[l, kind], device),
        ]

    def in_plane(self, l, kind, side, color):
        at = self.at
        w = self.w.at[self.block(l, kind), pl.ds(pl.multiple_of(self.share(at.core, color) + side * PART, 16), PART)]
        return remote(w, w, self.ps[0].at[l, kind, side], self.ps[1].at[l, kind, side], at.beside(side))

    def to_sibling(self, l, kind, core, color, which):
        w = self.w.at[self.block(l, kind), pl.ds(self.share(core, color), SHARE)]
        return remote(w, w, self.cs[0].at[l, kind, which], self.cs[1].at[l, kind, which], self.at.sibling())

    def small_to_sibling(self, l, kind, core):
        small = self.small_ref.at[self.block(l, kind), pl.ds(pl.multiple_of(core * 32, 32), 32)]
        return remote(small, small, self.small_cs[0].at[l, kind], self.small_cs[1].at[l, kind], self.at.sibling())

    def begin(self, l):
        at = self.at
        for kind, k in ((0, 1), (1, -1)):
            for c in self.along_z(l, l * 4 + at.s, kind, at.up_z(k)):
                c.start()

    def spread(self, l, kind):
        at = self.at
        for side in range(4):
            self.in_plane(l, kind, side, at.color).start()
        self.to_sibling(l, kind, at.core, at.color, 0).start()
        self.small_to_sibling(l, kind, at.core).start()

    def near(self, l):
        at = self.at
        for kind, k in ((0, -1), (1, 1)):
            b = self.block(l, kind)
            for c in self.along_z(l, b, kind, at.up_z(k)):
                c.wait_recv()

            @pl.when(at.core == 1 - kind)
            def _():
                for c in self.along_z(l, b, 2, at.up_z(-k)):
                    c.start()
        for kind in range(2):
            self.spread(l, kind)

    def close_plane(self, l, kind):
        at = self.at
        for side in range(4):
            self.in_plane(l, kind, side, 1 - at.color).wait_recv()
        self.to_sibling(l, kind, at.core, 1 - at.color, 1).start()

    def far(self, l):
        at = self.at
        for c in self.along_z(l, self.block(l, 2), 2, at.up_z(1)):
            c.wait_recv()
        self.spread(l, 2)
        for kind in range(2):
            self.close_plane(l, kind)

    def last(self, l):
        at = self.at
        self.close_plane(l, 2)
        for kind in range(3):
            self.to_sibling(l, kind, 1 - at.core, at.color, 0).wait_recv()
            self.to_sibling(l, kind, 1 - at.core, 1 - at.color, 1).wait_recv()
            self.small_to_sibling(l, kind, 1 - at.core).wait_recv()

    def drain(self, l):
        at = self.at
        for kind in range(3):
            for c in self.along_z(l, self.block(l, kind), kind, at.up_z(1)):
                c.wait_send()
            for side in range(4):
                self.in_plane(l, kind, side, at.color).wait_send()
            self.to_sibling(l, kind, at.core, at.color, 0).wait_send()
            self.to_sibling(l, kind, at.core, 1 - at.color, 1).wait_send()
            self.small_to_sibling(l, kind, at.core).wait_send()


def gather_scratch():
    return pair(2, 3) + pair(2, 3, 4) + pair(2, 3, 2) + pair(2, 3) + pair(2, 3)


def make_gather(at, w_ref, small_ref, sems):
    return Gather(at, w_ref, small_ref, [tuple(sems[2 * i : 2 * i + 2]) for i in range(5)])


def clear(ref):
    ref[...] = jnp.zeros(ref.shape, ref.dtype)


def step_kernel(heights_ref, images_ref, cot_ref, up_in, down_in, small_in, up_out, down_out, small_out, w_ref, small_ref, image_ref, v_ref, pad_ref, shift_ref, mix_ref, x_ref, act_ref, slope_ref, xhat_ref, inv_ref, proj_ref, dk_ref, sg_ref, g_ref, load_sem, own_sem, *refs):
    at = Place()
    gather = make_gather(at, w_ref, small_ref, refs[:10])
    red = make_reduce(at, w_ref, (up_out, down_out, small_out), refs[10:])
    own = [[], []]
    for l in range(2):
        b = l * 4 + at.s
        for t in range(10):
            lanes = pl.ds(128 * t, 128)
            own[l].append(pltpu.make_async_copy(up_in.at[l, :, lanes], w_ref.at[b, pl.ds(C * t, C)], own_sem.at[l, t]))
            own[l].append(pltpu.make_async_copy(down_in.at[l, :, lanes], w_ref.at[b, pl.ds(3200 + C * t, C)], own_sem.at[l, 10 + t]))
        own[l].append(pltpu.make_async_copy(small_in.at[l], small_ref.at[b], own_sem.at[l, 20]))
    load = [pltpu.make_async_copy(images_ref.at[at.s, 0], image_ref.at[0], load_sem.at[0]), pltpu.make_async_copy(cot_ref.at[at.s, 0], image_ref.at[1], load_sem.at[1])]
    for c in own[0] + own[1] + load:
        c.start()
    greet([at.sibling()] + [at.first(k)[1] for k in (1, 2, 3)] + [at.second(k)[1] for k in (1, 2, 3)] + [at.up_z(k) for k in range(1, 8)])
    for c in own[0]:
        c.wait()
    gather.begin(0)
    clear(pad_ref)
    clear(x_ref)
    clear(sg_ref)
    h = heights_ref[at.s]
    for c in load + own[1]:
        c.wait()
    v_ref[0] = (image_ref[0].astype(F32).reshape(CELLS, C) * window_of(h)).astype(BF)
    gather.near(0)
    gather.begin(1)
    gather.far(0)
    gather.last(0)

    def forward(b, _):
        v_ref[b + 1] = block_forward(b, h, w_ref, small_ref, v_ref, pad_ref, shift_ref, mix_ref, act_ref, slope_ref, xhat_ref, inv_ref, proj_ref)
        for n, part in ((1, gather.near), (2, gather.far), (3, gather.last)):
            @pl.when(b == n)
            def _():
                part(1)
        return 0

    lax.fori_loop(0, NB, forward, 0)
    gather.drain(0)
    gather.drain(1)
    g_ref[...] = image_ref[1].astype(F32).reshape(CELLS, C)
    stages = red.stages()

    def tick(t, _):
        b = NB - 1 - t

        @pl.when(b >= 0)
        def _():
            w_ref[b, 6592:6656, :] = jnp.zeros((64, 128), BF)
            g_ref[...] = block_backward(b, h, g_ref[...], w_ref, small_ref, v_ref, pad_ref, shift_ref, mix_ref, x_ref, act_ref, slope_ref, xhat_ref, inv_ref, proj_ref, dk_ref, sg_ref)
        for n, stage in enumerate(stages):
            @pl.when((b + n >= 0) & (b + n < NB))
            def _():
                stage(b + n)
        return 0

    lax.fori_loop(0, NB + len(stages) - 1, tick, 0)


def step(heights, images, cotangent, up, down, small):
    hbm = pl.BlockSpec(memory_space=pl.ANY)
    vm = pl.BlockSpec(memory_space=pltpu.VMEM)
    scratch = [
        pltpu.VMEM((NB, ROWS, 128), BF),
        pltpu.VMEM((NB, 64, CP), F32),
        pltpu.VMEM((2, SIDE, SIDE, C), BF),
        pltpu.VMEM((NB + 1, CELLS, C), BF),
        pltpu.VMEM((SIDE, 32, CP), F32),
        pltpu.VMEM((7, SIDE, SIDE, CP), F32),
        pltpu.VMEM((SIDE, SIDE, CP), F32),
        pltpu.VMEM((SIDE, SIDE, CP), F32),
        pltpu.VMEM((NB, CELLS, HID), BF),
        pltpu.VMEM((NB, CELLS, HID), BF),
        pltpu.VMEM((NB, CELLS, C), F32),
        pltpu.VMEM((NB, CELLS, 1), F32),
        pltpu.VMEM((NB, CELLS, C), BF),
        pltpu.VMEM((49, 8, CP), F32),
        pltpu.VMEM((64, CP), F32),
        pltpu.VMEM((CELLS, C), F32),
        pltpu.SemaphoreType.DMA((2,)),
        pltpu.SemaphoreType.DMA((2, 21)),
    ]
    return pl.pallas_call(
        step_kernel,
        out_shape=(jax.ShapeDtypeStruct((2, C, HID), BF), jax.ShapeDtypeStruct((2, C, HID), BF), jax.ShapeDtypeStruct((2, 64, CP), F32)),
        in_specs=[pl.BlockSpec(memory_space=pltpu.SMEM)] + [hbm] * 5,
        out_specs=(vm, vm, vm),
        scratch_shapes=scratch + gather_scratch() + reduce_scratch(),
        compiler_params=pltpu.CompilerParams(collective_id=0, has_side_effects=True, vmem_limit_bytes=62 * 2**20),
        cost_estimate=pl.CostEstimate(flops=12 * 10**9, bytes_accessed=30 * 10**6, transcendentals=3 * 10**6),
    )(heights, images, cotangent, up, down, small)


def body(images, cotangent, heights, dw_kernel, dw_bias, norm_gain, norm_bias, up_weight, up_bias, down_weight, down_bias, layer_scale):
    small = pack_small(*(a[:, 0] for a in (dw_kernel, dw_bias, norm_gain, norm_bias, up_bias, down_bias, layer_scale)))
    up, down, small = step(heights, images, cotangent, up_weight[:, 0], down_weight[:, 0].swapaxes(1, 2), small)
    row = lambda i: small[:, i, :C]
    up_bias_grad = small[:, 54:58].reshape(2, 4 * CP)[:, :HID]
    parts = (small[:, :49, :C].reshape(2, 7, 7, C), row(49), row(50), row(51), up, up_bias_grad, down.swapaxes(1, 2), row(52), row(53))
    return tuple(p[:, None] for p in parts)


def solution(mesh):
    three, two = P(None, "section", None, None), P(None, "section", None)
    five = P(None, "section", None, None, None)
    image = P(None, "dp", None, None, None)
    weights = (five, two, two, two, three, two, three, two, two)
    return jax.shard_map(body, mesh=mesh, in_specs=(image, image, P()) + weights, out_specs=weights, check_vma=False)
```

time: 312 us -> 185 us (0.59)
  Pallas kernels: 285 us -> 172 us
  local copies, waits for them, and re-layouts: 22 us -> 11.5 us
  other arithmetic: 4.07 us -> 0.76 us
    pallas_call x3 -> x1, Pallas kernels: 285 us -> 172 us  [step(): pl.pallas_call(step_kernel, out_shape=(jax.ShapeDtypeStruct((2, C, HID),...]
    reshape x4 -> x0, local copies, waits for them, and re-layouts: 5.62 us -> none  [the longest x1 2.71 us: unpack(): fin[:, :3200].reshape(2, 10, C, 128).transpose(0, 2, 1, 3)]
    concatenate x1 -> x0, other arithmetic: 3.31 us -> none  [body(): jnp.concatenate([up_weight[:, 0], down_weight[:, 0].swapaxes(1, 2)], axis=1)]
    dynamic_slice x2 -> x0, local copies, waits for them, and re-layouts: 3.16 us -> none  [the longest x1 1.8 us: body(): lax.dynamic_index_in_dim(a[:, 0], s, 0, keepdims=False).reshape(CELLS, C)]
where the time goes in v2:
time: 185 us
  Pallas kernels  172 us (93%)
  local copies, waits for them, and re-layouts  11.5 us (6%)
    pallas_call x1, Pallas kernels, step(): pl.pallas_call(step_kernel, out_shape=(jax.ShapeDtypeStruct((2, C, HID),...  172 us
    unnamed x9, local copies, waits for them, and re-layouts  7.32 us

profile of v2, /device:TPU:1, one launch (start us, length us, event | category | flops | bytes accessed | tf_op | source)
XLA Modules:
  0.0 185.0 jit_solution(4769401699564128064)
XLA Ops:
  0.6 1.0 copy.24
  1.7 0.8 concatenate.6
  2.5 0.7 copy.33
  3.2 0.1 pad.12.clone
  3.3 0.8 fusion.small_in
  4.0 172.1 %shard_map.187 = (bf16[2,320,1280]{2,1,0:T(8,128)(2,1)}, bf16[2,320,1280]{2,1,0:T(8,128)(2,1)}, f32[2,64,384]{2,1,0:T(8,128)}) custom-call(s32[4]{0:T(128)} %heights_ref.1, bf16[4,1,16,16,320]{4,3,2,1,0:T(8,128)(2,1)} %images_ref.1, bf16[4,1,16,16,320]{4,3,2,1,0:T(8,128)(2,1)} %cot_ref.1, bf16[2,320,1280]{2,1,0:T(8,128)(2,1)} %bitcast.26, ...), custom_call_target="tpu_custom_call" | custom-call | flops 12000000000 | bytes 30000000 | tf_op jit(solution)/shard_map/pallas_call | solution.py:628
  176.1 1.6 fusion.1
  177.7 0.9 slice.24
  178.7 0.1 copy.26
  178.7 0.8 copy.27
  179.6 0.8 slice_bitcast_fusion
  180.4 0.6 broadcast_in_dim.14
  181.0 0.0 copy-start
  181.0 2.8 %copy.36 = bf16[2,1,320,1280]{3,2,1,0:T(8,128)(2,1)} copy(bf16[2,1,320,1280]{3,2,1,0:T(8,128)(2,1)} %bitcast.21) | data formatting | bytes 3276800
  183.8 0.0 copy-done
  183.8 1.2 copy.37
  (6 shorter events, 0.1 us)
Async XLA Ops:
  181.0 2.8 %copy-start = (bf16[2,320,1280]{2,1,0:T(8,128)(2,1)S(1)}, bf16[2,320,1280]{2,1,0:T(8,128)(2,1)}, u32[]{:S(2)}) copy-start(bf16[2,320,1280]{2,1,0:T(8,128)(2,1)} %get-tuple-element.14) | copy-start | bytes 4915204

commit v3 on v2

--- a/solution.py
+++ b/solution.py
@@ -9,6 +9,7 @@
 CP = 384
 CELLS = SIDE * SIDE
 ROWS = 6656
+DOWN, UP, SMALL = 0, 3200, 6400
 BF, F32 = jnp.bfloat16, jnp.float32
 K0, K1 = 0.7978845608028654, 0.044715
 T_LANES = (((1,), (1,)), ((), ()))
@@ -122,7 +123,7 @@
     proj = jnp.broadcast_to(small_row(small_ref, b, 52), (CELLS, C))
     for n in range(5):
         cols = slice(256 * n, 256 * n + 256)
-        u = dot(normed, weight_chunk(w_ref, b, 0, n)) + up_bias_chunk(small_ref, b, n)
+        u = dot(normed, weight_chunk(w_ref, b, UP, n)) + up_bias_chunk(small_ref, b, n)
         uu = u * u
         t = jnp.tanh(u * (K0 + (K0 * K1) * uu))
         lift = 0.5 + 0.5 * t
@@ -130,14 +131,15 @@
         slope = lift + (u * (0.5 - 0.5 * t * t)) * (K0 + (3 * K0 * K1) * uu)
         act_ref[b, :, cols] = act
         slope_ref[b, :, cols] = slope.astype(BF)
-        proj = proj + dot(act, weight_chunk(w_ref, b, 3200, n), T_LANES)
+        proj = proj + dot(act, weight_chunk(w_ref, b, DOWN, n), T_LANES)
     proj_ref[b] = proj.astype(BF)
     out = (v + small_row(small_ref, b, 53) * proj) * window_of(h)
     return out.astype(BF)
 
 
-def block_backward(b, h, g, w_ref, small_ref, v_ref, pad_ref, shift_ref, mix_ref, x_ref, act_ref, slope_ref, xhat_ref, inv_ref, proj_ref, dk_ref, sg_ref):
-    g = g * window_of(h)
+def products_backward(b, h, g_ref, w_ref, small_ref, pad_ref, act_ref, slope_ref, xhat_ref, inv_ref, proj_ref, sg_ref):
+    g = g_ref[...] * window_of(h)
+    g_ref[...] = g
     sg_ref[53:54, 0:C] = jnp.sum(g * proj_ref[b].astype(F32), axis=0, keepdims=True)
     dproj = g * small_row(small_ref, b, 53)
     sg_ref[52:53, 0:C] = jnp.sum(dproj, axis=0, keepdims=True)
@@ -148,19 +150,19 @@
     dnormed = None
     for n in range(5):
         cols = slice(256 * n, 256 * n + 256)
-        dact = dot(dproj, weight_chunk(w_ref, b, 3200, n))
+        dact = dot(dproj, weight_chunk(w_ref, b, DOWN, n))
         dhid = dact * slope_ref[b, :, cols].astype(F32)
         bias = jnp.sum(dhid, axis=0, keepdims=True)
         dhid = dhid.astype(BF)
-        part = dot(dhid, weight_chunk(w_ref, b, 0, n), T_LANES)
+        part = dot(dhid, weight_chunk(w_ref, b, UP, n), T_LANES)
         dnormed = part if dnormed is None else dnormed + part
         dup = dot(normed, dhid, T_ROWS).astype(BF)
         ddown = dot(dproj, act_ref[b, :, cols], T_ROWS).astype(BF)
         for k in range(2):
             t = 2 * n + k
             lanes = slice(128 * k, 128 * k + 128)
-            w_ref[b, 320 * t : 320 * t + 320, :] = dup[:, lanes]
-            w_ref[b, 3200 + 320 * t : 3520 + 320 * t, :] = ddown[:, lanes]
+            w_ref[b, UP + C * t : UP + C * t + C, :] = dup[:, lanes]
+            w_ref[b, DOWN + C * t : DOWN + C * t + C, :] = ddown[:, lanes]
             sg_ref[54 + t // 3 : 55 + t // 3, (t % 3) * 128 : (t % 3 + 1) * 128] = bias[:, lanes]
     sg_ref[50:51, 0:C] = jnp.sum(dnormed * xhat, axis=0, keepdims=True)
     sg_ref[51:52, 0:C] = jnp.sum(dnormed, axis=0, keepdims=True)
@@ -170,17 +172,16 @@
     dmixed = inv_ref[b] * (dxhat - m0 - xhat * m1)
     sg_ref[49:50, 0:C] = jnp.sum(dmixed, axis=0, keepdims=True)
     pad_ref[:, 8:24, 0:C] = dmixed.reshape(SIDE, SIDE, C)
+
+
+def spatial_backward(b, g_ref, w_ref, small_ref, v_ref, pad_ref, shift_ref, mix_ref, x_ref, dk_ref, sg_ref):
     x_ref[:, :, 0:C] = v_ref[b].astype(F32).reshape(SIDE, SIDE, C)
     shift_columns(pad_ref, shift_ref, 11, -1)
     conv_backward(shift_ref, x_ref, small_ref, b, mix_ref, dk_ref)
     sg_ref[0:49, :] = jnp.sum(dk_ref[...], axis=1)
     for j in range(3):
-        w_ref[b, 6400 + 64 * j : 6464 + 64 * j, :] = sg_ref[:, 128 * j : 128 * j + 128].astype(BF)
-    return (g + mix_ref[:, :, 0:C].reshape(CELLS, C)).astype(BF).astype(F32)
-
-
-def clear(ref):
-    ref[...] = jnp.zeros(ref.shape, ref.dtype)
+        w_ref[b, SMALL + 64 * j : SMALL + 64 * j + 64, :] = sg_ref[:, 128 * j : 128 * j + 128].astype(BF)
+    g_ref[...] = (g_ref[...] + mix_ref[:, :, 0:C].reshape(CELLS, C)).astype(BF).astype(F32)
 
 
 def pack_small(dw_kernel, dw_bias, gain, nbias, up_bias, down_bias, scale):
@@ -191,7 +192,6 @@
     return jnp.concatenate([rows, up, jnp.zeros((n, 6, CP), F32)], axis=1)
 
 
-HALF, QUART, PIECE = ROWS // 2, ROWS // 8, ROWS // 32
 MESH = pl.DeviceIdType.MESH
 
 
@@ -205,7 +205,6 @@
         self.step2 = 10 - self.step1
         self.f1 = (d // self.step1) % 4
         self.f2 = (d // self.step2) % 4
-        self.half = pl.multiple_of(self.core * HALF, HALF)
         self.x, self.y = (d // 2) % 4, (d // 8) % 4
         self.color = (self.x + self.y) % 2
 
@@ -241,108 +240,123 @@
     return pltpu.make_async_remote_copy(src_ref=src, dst_ref=dst, send_sem=send, recv_sem=recv, device_id=device, device_id_type=MESH)
 
 
-def add_into(dst_ref, b, base, count, src_refs):
-    def step(i, _):
-        rows = pl.ds(pl.multiple_of(base + i * PIECE, 16), PIECE)
-        own = pl.ds(pl.multiple_of(i * PIECE, 16), PIECE)
+def add_rows(dst_ref, b, base, count, src_refs):
+    step = next(n for n in (256, 224, 208, 192, 112, 96) if count % n == 0)
+
+    def add(i, _):
+        rows = pl.ds(pl.multiple_of(base + i * step, 16), step)
+        own = pl.ds(pl.multiple_of(i * step, 16), step)
         total = dst_ref[b, rows, :].astype(F32)
         for src in src_refs:
             total = total + src[own, :].astype(F32)
         dst_ref[b, rows, :] = total.astype(BF)
         return 0
 
-    lax.fori_loop(0, count, step, 0)
+    lax.fori_loop(0, count // step, add, 0)
 
 
 class Reduce:
-    def __init__(self, at, g_ref, outs, fin_ref, cr, xr, yr, zr, sems):
-        self.at, self.g, self.fin = at, g_ref, fin_ref
+    def __init__(self, at, part, g_ref, outs, fin_ref, cr, xr, yr, zr, sems):
+        self.at, self.part, self.g, self.fin = at, part, g_ref, fin_ref
         self.up, self.down, self.small = outs
         self.cr, self.xr, self.yr, self.zr = cr, xr, yr, zr
         self.sems = sems
+        self.start = 3072 * part
+        self.half = 1536 + 256 * part
+        self.quarter, self.piece_rows = self.half // 4, self.half // 16
+        self.side = self.quarter // 2
+        self.mine = self.start + at.core * self.half
+
+    def rows(self, at, count):
+        return pl.ds(pl.multiple_of(at, 16), count)
 
     def core_copy(self, b):
-        at, (cs, crs) = self.at, self.sems[0]
-        other = pl.multiple_of((1 - at.core) * HALF, HALF)
-        return remote(self.g.at[b, pl.ds(other, HALF)], self.cr.at[b], cs.at[b], crs.at[b], at.sibling())
-
-    def first_copy(self, b, k):
-        at, (xs, xrs) = self.at, self.sems[1]
-        q, device = at.first(k)
-        rows = pl.ds(pl.multiple_of(at.half + q * QUART, 16), QUART)
-        return remote(self.g.at[b, rows], self.xr.at[b, k - 1], xs.at[b, k - 1], xrs.at[b, k - 1], device)
+        at, (s, r) = self.at, self.sems[0]
+        other = self.start + (1 - at.core) * self.half
+        return remote(self.g.at[b, self.rows(other, self.half)], self.cr.at[b, pl.ds(self.start // 2, self.half)], s.at[self.part, b], r.at[self.part, b], at.sibling())
+
+    def first_copy(self, b, n):
+        at, (s, r) = self.at, self.sems[1]
+        quarter, high, k = ((2, 0, 1), (2, 1, 3), (1, 1, 1), (3, 0, 3), (1, 0, 1), (3, 1, 3))[n]
+        rows = self.rows(self.mine + ((at.f1 + quarter) % 4) * self.quarter + high * self.side, self.side)
+        return remote(self.g.at[b, rows], self.xr.at[b, n, pl.ds(192 * self.part, self.side)], s.at[self.part, b, n], r.at[self.part, b, n], at.first(k)[1])
 
     def second_copy(self, b, k):
-        at, (ys, yrs) = self.at, self.sems[2]
+        at, (s, r) = self.at, self.sems[2]
         q, device = at.second(k)
-        rows = pl.ds(pl.multiple_of(at.half + at.f1 * QUART + q * PIECE, 16), PIECE)
-        return remote(self.g.at[b, rows], self.yr.at[b, k - 1], ys.at[b, k - 1], yrs.at[b, k - 1], device)
+        rows = self.rows(self.mine + at.f1 * self.quarter + q * self.piece_rows, self.piece_rows)
+        return remote(self.g.at[b, rows], self.yr.at[b, k - 1, pl.ds(96 * self.part, self.piece_rows)], s.at[self.part, b, k - 1], r.at[self.part, b, k - 1], device)
 
     def piece(self):
         at = self.at
-        return pl.multiple_of(at.half + at.f1 * QUART + at.f2 * PIECE, 16)
+        return self.rows(self.mine + at.f1 * self.quarter + at.f2 * self.piece_rows, self.piece_rows)
 
     def z_copy(self, b, hi, source):
-        at, (zs, zrs) = self.at, self.sems[3]
+        at, (s, r) = self.at, self.sems[3]
         device = (b % 4, hi * 32 + at.d % 32)
-        return remote(self.g.at[b, pl.ds(self.piece(), PIECE)], self.zr.at[b // 4, source], zs.at[b, hi], zrs.at[b // 4, source], device)
-
-    def back_second(self, l, k):
+        return remote(self.g.at[b, self.piece()], self.zr.at[b // 4, source, pl.ds(96 * self.part, self.piece_rows)], s.at[self.part, b, hi], r.at[self.part, b // 4, source], device)
+
+    def back_second(self, l, k, arriving):
         at, (s, r) = self.at, self.sems[4]
-        _, device = at.second(k)
-        rows = pl.ds(self.piece(), PIECE)
-        return remote(self.fin.at[l, rows], self.fin.at[l, rows], s.at[l, k - 1], r.at[l, k - 1], device)
-
-    def back_second_in(self, l, k):
-        at, (s, r) = self.at, self.sems[4]
-        q, device = at.second(4 - k)
-        rows = pl.ds(pl.multiple_of(at.half + at.f1 * QUART + q * PIECE, 16), PIECE)
-        return remote(self.fin.at[l, rows], self.fin.at[l, rows], s.at[l, k - 1], r.at[l, k - 1], device)
-
-    def back_first(self, l, k):
+        device = at.second(k)[1]
+        q = at.second(4 - k)[0] if arriving else at.f2
+        rows = self.fin.at[l, self.rows(self.mine + at.f1 * self.quarter + q * self.piece_rows, self.piece_rows)]
+        return remote(rows, rows, s.at[self.part, l, k - 1], r.at[self.part, l, k - 1], device)
+
+    def back_first(self, l, k, arriving):
         at, (s, r) = self.at, self.sems[5]
-        _, device = at.first(k)
-        rows = pl.ds(pl.multiple_of(at.half + at.f1 * QUART, 16), QUART)
-        return remote(self.fin.at[l, rows], self.fin.at[l, rows], s.at[l, k - 1], r.at[l, k - 1], device)
-
-    def back_first_in(self, l, k):
-        at, (s, r) = self.at, self.sems[5]
-        q, device = at.first(4 - k)
-        rows = pl.ds(pl.multiple_of(at.half + q * QUART, 16), QUART)
-        return remote(self.fin.at[l, rows], self.fin.at[l, rows], s.at[l, k - 1], r.at[l, k - 1], device)
+        device = at.first(k)[1]
+        q = at.first(4 - k)[0] if arriving else at.f1
+        rows = self.fin.at[l, self.rows(self.mine + q * self.quarter, self.quarter)]
+        return remote(rows, rows, s.at[self.part, l, k - 1], r.at[self.part, l, k - 1], device)
 
     def back_core(self, l, core):
         at, (s, r) = self.at, self.sems[6]
-        rows = pl.ds(pl.multiple_of(core * HALF, HALF), HALF)
-        return remote(self.fin.at[l, rows], self.fin.at[l, rows], s.at[l], r.at[l], at.sibling())
+        rows = self.fin.at[l, self.rows(self.start + core * self.half, self.half)]
+        return remote(rows, rows, s.at[self.part, l], r.at[self.part, l], at.sibling())
 
     def stage0(self, b):
         self.core_copy(b).start()
 
     def stage1(self, b):
         self.core_copy(b).wait()
-        add_into(self.g, b, self.at.half, 16, [self.cr.at[b]])
-        for k in (2, 1, 3):
-            self.first_copy(b, k).start()
+        add_rows(self.g, b, self.mine, self.half, [self.cr.at[b, pl.ds(self.start // 2, self.half)]])
+        for n in range(4):
+            self.first_copy(b, n).start()
 
     def stage2(self, b):
-        for k in (1, 2, 3):
-            self.first_copy(b, k).wait()
-        add_into(self.g, b, self.at.half + self.at.f1 * QUART, 4, [self.xr.at[b, k] for k in range(3)])
+        at = self.at
+        for n in range(2):
+            self.first_copy(b, n).wait_recv()
+            quarter, high = ((1, 0), (3, 1))[n]
+            base = self.mine + ((at.f1 + quarter) % 4) * self.quarter + high * self.side
+            add_rows(self.g, b, base, self.side, [self.xr.at[b, n, pl.ds(192 * self.part, self.side)]])
+            self.first_copy(b, 4 + n).start()
+
+    def stage3(self, b):
+        at = self.at
+        for n in range(6):
+            self.first_copy(b, n).wait_send()
+        for n in range(2, 6):
+            self.first_copy(b, n).wait_recv()
+        base = self.mine + at.f1 * self.quarter
+        for high, (one, two) in enumerate(((3, 4), (2, 5))):
+            add_rows(self.g, b, base + high * self.side, self.side, [self.xr.at[b, n, pl.ds(192 * self.part, self.side)] for n in (one, two)])
         for k in (2, 1, 3):
             self.second_copy(b, k).start()
 
-    def stage3(self, b):
+    def stage4(self, b):
         at = self.at
         for k in (1, 2, 3):
             self.second_copy(b, k).wait()
-        add_into(self.g, b, self.piece(), 1, [self.yr.at[b, k] for k in range(3)])
+        base = self.mine + at.f1 * self.quarter + at.f2 * self.piece_rows
+        add_rows(self.g, b, base, self.piece_rows, [self.yr.at[b, k, pl.ds(96 * self.part, self.piece_rows)] for k in range(3)])
         for hi in range(2):
             @pl.when(at.z != hi * 4 + b % 4)
             def _():
                 self.z_copy(b, hi, at.z).start()
 
-    def stage4(self, b):
+    def stage5(self, b):
         at = self.at
         for hi in range(2):
             @pl.when(at.z != hi * 4 + b % 4)
@@ -354,39 +368,37 @@
             l = b // 4
             for k in range(1, 8):
                 self.z_copy(b, 0, (at.z + k) % 8).wait_recv()
-            rows = pl.ds(self.piece(), PIECE)
-            self.zr[l, at.z] = self.g[b, rows, :]
-            total = self.zr[l, 0].astype(F32)
+            rows = pl.ds(96 * self.part, self.piece_rows)
+            self.zr[l, at.z, rows, :] = self.g[b, self.piece(), :]
+            total = self.zr[l, 0, rows, :].astype(F32)
             for z in range(1, 8):
-                total = total + self.zr[l, z].astype(F32)
-            self.fin[l, rows, :] = total.astype(BF)
+                total = total + self.zr[l, z, rows, :].astype(F32)
+            self.fin[l, self.piece(), :] = total.astype(BF)
             for k in (2, 1, 3):
-                self.back_second(l, k).start()
-
-    def stage5(self, b):
+                self.back_second(l, k, False).start()
+
+    def stage6(self, b):
+        @pl.when(self.at.s == b % 4)
+        def _():
+            l = b // 4
+            for k in (1, 2, 3):
+                self.back_second(l, k, False).wait_send()
+                self.back_second(l, k, True).wait_recv()
+            for k in (2, 1, 3):
+                self.back_first(l, k, False).start()
+
+    def stage7(self, b):
         at = self.at
 
         @pl.when(at.s == b % 4)
         def _():
             l = b // 4
             for k in (1, 2, 3):
-                self.back_second(l, k).wait_send()
-                self.back_second_in(l, k).wait_recv()
-            for k in (2, 1, 3):
-                self.back_first(l, k).start()
-
-    def stage6(self, b):
-        at = self.at
-
-        @pl.when(at.s == b % 4)
-        def _():
-            l = b // 4
-            for k in (1, 2, 3):
-                self.back_first(l, k).wait_send()
-                self.back_first_in(l, k).wait_recv()
+                self.back_first(l, k, False).wait_send()
+                self.back_first(l, k, True).wait_recv()
             self.back_core(l, at.core).start()
 
-    def stage7(self, b):
+    def stage8(self, b):
         at = self.at
 
         @pl.when(at.s == b % 4)
@@ -394,19 +406,17 @@
             l = b // 4
             self.back_core(l, at.core).wait_send()
             self.back_core(l, 1 - at.core).wait_recv()
+            if self.part == 0:
+                return
             for t in range(10):
                 lanes = slice(128 * t, 128 * t + 128)
-                self.up[l, :, lanes] = self.fin[l, C * t : C * t + C, :]
-                self.down[l, :, lanes] = self.fin[l, 3200 + C * t : 3200 + C * t + C, :]
+                self.up[l, :, lanes] = self.fin[l, UP + C * t : UP + C * t + C, :]
+                self.down[l, :, lanes] = self.fin[l, DOWN + C * t : DOWN + C * t + C, :]
             for t in range(3):
-                self.small[l, :, 128 * t : 128 * t + 128] = self.fin[l, 6400 + 64 * t : 6464 + 64 * t, :].astype(F32)
+                self.small[l, :, 128 * t : 128 * t + 128] = self.fin[l, SMALL + 64 * t : SMALL + 64 * t + 64, :].astype(F32)
 
     def stages(self):
-        return [self.stage0, self.stage1, self.stage2, self.stage3, self.stage4, self.stage5, self.stage6, self.stage7]
-
-
-def reduce_partners(at):
-    return [at.sibling()] + [at.first(k)[1] for k in (1, 2, 3)] + [at.second(k)[1] for k in (1, 2, 3)] + [at.up_z(k) for k in range(1, 8)]
+        return [self.stage0, self.stage1, self.stage2, self.stage3, self.stage4, self.stage5, self.stage6, self.stage7, self.stage8]
 
 
 def pair(*shape):
@@ -416,20 +426,20 @@
 def reduce_scratch():
     buffers = [
         pltpu.VMEM((2, ROWS, 128), BF),
-        pltpu.VMEM((NB, HALF, 128), BF),
-        pltpu.VMEM((NB, 3, QUART, 128), BF),
-        pltpu.VMEM((NB, 3, PIECE, 128), BF),
-        pltpu.VMEM((2, 8, PIECE, 128), BF),
+        pltpu.VMEM((NB, ROWS // 2, 128), BF),
+        pltpu.VMEM((NB, 6, ROWS // 16, 128), BF),
+        pltpu.VMEM((NB, 3, ROWS // 32, 128), BF),
+        pltpu.VMEM((2, 8, ROWS // 32, 128), BF),
     ]
-    sems = pair(NB) + pair(NB, 3) + pair(NB, 3)
-    sems += [pltpu.SemaphoreType.DMA((NB, 2)), pltpu.SemaphoreType.DMA((2, 8))]
-    sems += pair(2, 3) + pair(2, 3) + pair(2)
+    sems = pair(2, NB) + pair(2, NB, 6) + pair(2, NB, 3)
+    sems += [pltpu.SemaphoreType.DMA((2, NB, 2)), pltpu.SemaphoreType.DMA((2, 2, 8))]
+    sems += pair(2, 2, 3) + pair(2, 2, 3) + pair(2, 2)
     return buffers + sems
 
 
-def make_reduce(at, g_ref, outs, refs):
+def make_reduce(at, part, g_ref, outs, refs):
     sems = [tuple(refs[5 + 2 * i : 7 + 2 * i]) for i in range(7)]
-    return Reduce(at, g_ref, outs, *refs[:5], sems)
+    return Reduce(at, part, g_ref, outs, *refs[:5], sems)
 
 
 WHALF, SHARE, PART = 3200, 1600, 400
@@ -544,14 +554,14 @@
 def step_kernel(heights_ref, images_ref, cot_ref, up_in, down_in, small_in, up_out, down_out, small_out, w_ref, small_ref, image_ref, v_ref, pad_ref, shift_ref, mix_ref, x_ref, act_ref, slope_ref, xhat_ref, inv_ref, proj_ref, dk_ref, sg_ref, g_ref, load_sem, own_sem, *refs):
     at = Place()
     gather = make_gather(at, w_ref, small_ref, refs[:10])
-    red = make_reduce(at, w_ref, (up_out, down_out, small_out), refs[10:])
+    units = [make_reduce(at, part, w_ref, (up_out, down_out, small_out), refs[10:]) for part in range(2)]
     own = [[], []]
     for l in range(2):
         b = l * 4 + at.s
         for t in range(10):
             lanes = pl.ds(128 * t, 128)
-            own[l].append(pltpu.make_async_copy(up_in.at[l, :, lanes], w_ref.at[b, pl.ds(C * t, C)], own_sem.at[l, t]))
-            own[l].append(pltpu.make_async_copy(down_in.at[l, :, lanes], w_ref.at[b, pl.ds(3200 + C * t, C)], own_sem.at[l, 10 + t]))
+            own[l].append(pltpu.make_async_copy(up_in.at[l, :, lanes], w_ref.at[b, pl.ds(UP + C * t, C)], own_sem.at[l, t]))
+            own[l].append(pltpu.make_async_copy(down_in.at[l, :, lanes], w_ref.at[b, pl.ds(DOWN + C * t, C)], own_sem.at[l, 10 + t]))
         own[l].append(pltpu.make_async_copy(small_in.at[l], small_ref.at[b], own_sem.at[l, 20]))
     load = [pltpu.make_async_copy(images_ref.at[at.s, 0], image_ref.at[0], load_sem.at[0]), pltpu.make_async_copy(cot_ref.at[at.s, 0], image_ref.at[1], load_sem.at[1])]
     for c in own[0] + own[1] + load:
@@ -584,22 +594,34 @@
     gather.drain(0)
     gather.drain(1)
     g_ref[...] = image_ref[1].astype(F32).reshape(CELLS, C)
-    stages = red.stages()
+    stages = [unit.stages() for unit in units]
+    depth = len(stages[0])
+
+    def run_stages(t, first):
+        for n in range(depth):
+            ago = n - first
+            b = NB - 1 - t + (ago + 1) // 2
+
+            @pl.when((b >= 0) & (b < NB))
+            def _():
+                stages[ago % 2][n](b)
 
     def tick(t, _):
         b = NB - 1 - t
 
         @pl.when(b >= 0)
         def _():
-            w_ref[b, 6592:6656, :] = jnp.zeros((64, 128), BF)
-            g_ref[...] = block_backward(b, h, g_ref[...], w_ref, small_ref, v_ref, pad_ref, shift_ref, mix_ref, x_ref, act_ref, slope_ref, xhat_ref, inv_ref, proj_ref, dk_ref, sg_ref)
-        for n, stage in enumerate(stages):
-            @pl.when((b + n >= 0) & (b + n < NB))
-            def _():
-                stage(b + n)
+            w_ref[b, ROWS - 64 : ROWS, :] = jnp.zeros((64, 128), BF)
+            products_backward(b, h, g_ref, w_ref, small_ref, pad_ref, act_ref, slope_ref, xhat_ref, inv_ref, proj_ref, sg_ref)
+        run_stages(t, 0)
+
+        @pl.when(b >= 0)
+        def _():
+            spatial_backward(b, g_ref, w_ref, small_ref, v_ref, pad_ref, shift_ref, mix_ref, x_ref, dk_ref, sg_ref)
+        run_stages(t, 1)
         return 0
 
-    lax.fori_loop(0, NB + len(stages) - 1, tick, 0)
+    lax.fori_loop(0, NB + depth // 2, tick, 0)
 
 
 def step(heights, images, cotangent, up, down, small):

time: 185 us -> 190 us (1.027)
  Pallas kernels: 172 us -> 176 us
    pallas_call x1, Pallas kernels: 172 us -> 176 us  [step(): pl.pallas_call(step_kernel, out_shape=(jax.ShapeDtypeStruct((2, C, HID),...]
where the time goes in v3:
time: 190 us; the launch traced here: 189 us
  Pallas kernels  176 us (93%)
  local copies, waits for them, and re-layouts  11.5 us (6%)
    pallas_call x1, Pallas kernels, step(): pl.pallas_call(step_kernel, out_shape=(jax.ShapeDtypeStruct((2, C, HID),...  176 us
    unnamed x9, local copies, waits for them, and re-layouts  7.32 us

profile of v3, /device:TPU:1, one launch (start us, length us, event | category | flops | bytes accessed | tf_op | source)
XLA Modules:
  0.0 189.4 jit_solution(3270117533971277220)
XLA Ops:
  0.6 1.0 copy.24
  1.7 0.8 concatenate.6
  2.5 0.7 copy.33
  3.2 0.1 pad.12.clone
  3.3 0.8 fusion.small_in
  4.0 176.5 %shard_map.187 = (bf16[2,320,1280]{2,1,0:T(8,128)(2,1)}, bf16[2,320,1280]{2,1,0:T(8,128)(2,1)}, f32[2,64,384]{2,1,0:T(8,128)}) custom-call(s32[4]{0:T(128)} %heights_ref.1, bf16[4,1,16,16,320]{4,3,2,1,0:T(8,128)(2,1)} %images_ref.1, bf16[4,1,16,16,320]{4,3,2,1,0:T(8,128)(2,1)} %cot_ref.1, bf16[2,320,1280]{2,1,0:T(8,128)(2,1)} %bitcast.26, ...), custom_call_target="tpu_custom_call" | custom-call | flops 12000000000 | bytes 30000000 | tf_op jit(solution)/shard_map/pallas_call | solution.py:650
  180.5 1.6 fusion.1
  182.2 0.9 slice.24
  183.1 0.1 copy.26
  183.2 0.8 copy.27
  184.0 0.8 slice_bitcast_fusion
  184.8 0.6 broadcast_in_dim.14
  185.4 0.0 copy-start
  185.4 2.8 %copy.36 = bf16[2,1,320,1280]{3,2,1,0:T(8,128)(2,1)} copy(bf16[2,1,320,1280]{3,2,1,0:T(8,128)(2,1)} %bitcast.21) | data formatting | bytes 3276800
  188.3 0.0 copy-done
  188.3 1.2 copy.37
  (6 shorter events, 0.1 us)
Async XLA Ops:
  185.4 2.8 %copy-start = (bf16[2,320,1280]{2,1,0:T(8,128)(2,1)S(1)}, bf16[2,320,1280]{2,1,0:T(8,128)(2,1)}, u32[]{:S(2)}) copy-start(bf16[2,320,1280]{2,1,0:T(8,128)(2,1)} %get-tuple-element.14) | copy-start | bytes 4915204

commit v4 on v3

--- a/solution.py
+++ b/solution.py
@@ -107,18 +107,20 @@
     return ((cell // SIDE < h) & (cell % SIDE < h)).astype(F32)
 
 
-def block_forward(b, h, w_ref, small_ref, v_ref, pad_ref, shift_ref, mix_ref, act_ref, slope_ref, xhat_ref, inv_ref, proj_ref):
-    v = v_ref[b].astype(F32)
-    pad_ref[:, 8:24, 0:C] = v.reshape(SIDE, SIDE, C)
+def spatial_forward(b, small_ref, v_ref, pad_ref, shift_ref, mix_ref, xhat_ref, inv_ref):
+    pad_ref[:, 8:24, 0:C] = v_ref[b].astype(F32).reshape(SIDE, SIDE, C)
     shift_columns(pad_ref, shift_ref, 5, 1)
     conv_forward(shift_ref, small_ref, b, mix_ref)
     mixed = mix_ref[:, :, 0:C].reshape(CELLS, C)
     center = jnp.sum(mixed, axis=1, keepdims=True) * (1.0 / C)
     mixed = mixed - center
     inv = lax.rsqrt(jnp.sum(mixed * mixed, axis=1, keepdims=True) * (1.0 / C) + 1e-6)
-    xhat = mixed * inv
-    xhat_ref[b] = xhat
+    xhat_ref[b] = mixed * inv
     inv_ref[b] = inv
+
+
+def products_forward(b, h, w_ref, small_ref, v_ref, act_ref, slope_ref, xhat_ref, proj_ref):
+    xhat = xhat_ref[b]
     normed = (xhat * small_row(small_ref, b, 50) + small_row(small_ref, b, 51)).astype(BF)
     proj = jnp.broadcast_to(small_row(small_ref, b, 52), (CELLS, C))
     for n in range(5):
@@ -133,8 +135,8 @@
         slope_ref[b, :, cols] = slope.astype(BF)
         proj = proj + dot(act, weight_chunk(w_ref, b, DOWN, n), T_LANES)
     proj_ref[b] = proj.astype(BF)
-    out = (v + small_row(small_ref, b, 53) * proj) * window_of(h)
-    return out.astype(BF)
+    out = (v_ref[b].astype(F32) + small_row(small_ref, b, 53) * proj) * window_of(h)
+    v_ref[b + 1] = out.astype(BF)
 
 
 def products_backward(b, h, g_ref, w_ref, small_ref, pad_ref, act_ref, slope_ref, xhat_ref, inv_ref, proj_ref, sg_ref):
@@ -255,6 +257,10 @@
     lax.fori_loop(0, count // step, add, 0)
 
 
+PACE_LATE = (0, 1, 3, 5, 7, 9, 10, 11, 12)
+PACE_EARLY = (0, 1, 3, 5, 7, 9, 13, 17, 19)
+
+
 class Reduce:
     def __init__(self, at, part, g_ref, outs, fin_ref, cr, xr, yr, zr, sems):
         self.at, self.part, self.g, self.fin = at, part, g_ref, fin_ref
@@ -457,13 +463,12 @@
         return pl.multiple_of(core * WHALF + color * SHARE, 16)
 
     def along_z(self, l, b, kind, device):
-        at = self.at
-        w = self.w.at[b, pl.ds(self.share(at.core, at.color), SHARE)]
-        small = self.small_ref.at[b, pl.ds(pl.multiple_of(at.core * 32, 32), 32)]
-        return [
-            remote(w, w, self.zs[0].at[l, kind], self.zs[1].at[l, kind], device),
-            remote(small, small, self.small_zs[0].at[l, kind], self.small_zs[1].at[l, kind], device),
-        ]
+        w = self.w.at[b, pl.ds(self.share(self.at.core, self.at.color), SHARE)]
+        return remote(w, w, self.zs[0].at[l, kind], self.zs[1].at[l, kind], device)
+
+    def small_along_z(self, l, b, kind, device):
+        small = self.small_ref.at[b, pl.ds(pl.multiple_of(self.at.core * 32, 32), 32)]
+        return remote(small, small, self.small_zs[0].at[l, kind], self.small_zs[1].at[l, kind], device)
 
     def in_plane(self, l, kind, side, color):
         at = self.at
@@ -481,28 +486,38 @@
     def begin(self, l):
         at = self.at
         for kind, k in ((0, 1), (1, -1)):
-            for c in self.along_z(l, l * 4 + at.s, kind, at.up_z(k)):
-                c.start()
+            self.small_along_z(l, l * 4 + at.s, kind, at.up_z(k)).start()
+        for kind, k in ((0, 1), (1, -1)):
+            self.along_z(l, l * 4 + at.s, kind, at.up_z(k)).start()
+
+    def relay(self, l, copy):
+        at = self.at
+        for kind, k in ((0, -1), (1, 1)):
+            b = self.block(l, kind)
+            copy(l, b, kind, at.up_z(k)).wait_recv()
+
+            @pl.when(at.core == 1 - kind)
+            def _():
+                copy(l, b, 2, at.up_z(-k)).start()
+
+    def small_ones(self, l):
+        at = self.at
+        self.small_along_z(l, self.block(l, 2), 2, at.up_z(1)).wait_recv()
+        self.small_to_sibling(l, 2, at.core).start()
+        for kind in range(3):
+            self.small_to_sibling(l, kind, 1 - at.core).wait_recv()
 
     def spread(self, l, kind):
         at = self.at
         for side in range(4):
             self.in_plane(l, kind, side, at.color).start()
         self.to_sibling(l, kind, at.core, at.color, 0).start()
-        self.small_to_sibling(l, kind, at.core).start()
 
     def near(self, l):
-        at = self.at
-        for kind, k in ((0, -1), (1, 1)):
-            b = self.block(l, kind)
-            for c in self.along_z(l, b, kind, at.up_z(k)):
-                c.wait_recv()
-
-            @pl.when(at.core == 1 - kind)
-            def _():
-                for c in self.along_z(l, b, 2, at.up_z(-k)):
-                    c.start()
+        self.relay(l, self.small_along_z)
+        self.relay(l, self.along_z)
         for kind in range(2):
+            self.small_to_sibling(l, kind, self.at.core).start()
             self.spread(l, kind)
 
     def close_plane(self, l, kind):
@@ -513,8 +528,7 @@
 
     def far(self, l):
         at = self.at
-        for c in self.along_z(l, self.block(l, 2), 2, at.up_z(1)):
-            c.wait_recv()
+        self.along_z(l, self.block(l, 2), 2, at.up_z(1)).wait_recv()
         self.spread(l, 2)
         for kind in range(2):
             self.close_plane(l, kind)
@@ -525,13 +539,12 @@
         for kind in range(3):
             self.to_sibling(l, kind, 1 - at.core, at.color, 0).wait_recv()
             self.to_sibling(l, kind, 1 - at.core, 1 - at.color, 1).wait_recv()
-            self.small_to_sibling(l, kind, 1 - at.core).wait_recv()
 
     def drain(self, l):
         at = self.at
         for kind in range(3):
-            for c in self.along_z(l, self.block(l, kind), kind, at.up_z(1)):
-                c.wait_send()
+            self.along_z(l, self.block(l, kind), kind, at.up_z(1)).wait_send()
+            self.small_along_z(l, self.block(l, kind), kind, at.up_z(1)).wait_send()
             for side in range(4):
                 self.in_plane(l, kind, side, at.color).wait_send()
             self.to_sibling(l, kind, at.core, at.color, 0).wait_send()
@@ -579,12 +592,17 @@
     v_ref[0] = (image_ref[0].astype(F32).reshape(CELLS, C) * window_of(h)).astype(BF)
     gather.near(0)
     gather.begin(1)
+    gather.small_ones(0)
+    spatial_forward(0, small_ref, v_ref, pad_ref, shift_ref, mix_ref, xhat_ref, inv_ref)
     gather.far(0)
     gather.last(0)
 
     def forward(b, _):
-        v_ref[b + 1] = block_forward(b, h, w_ref, small_ref, v_ref, pad_ref, shift_ref, mix_ref, act_ref, slope_ref, xhat_ref, inv_ref, proj_ref)
-        for n, part in ((1, gather.near), (2, gather.far), (3, gather.last)):
+        @pl.when(b > 0)
+        def _():
+            spatial_forward(b, small_ref, v_ref, pad_ref, shift_ref, mix_ref, xhat_ref, inv_ref)
+        products_forward(b, h, w_ref, small_ref, v_ref, act_ref, slope_ref, xhat_ref, proj_ref)
+        for n, part in ((0, gather.near), (2, gather.far), (2, gather.small_ones), (3, gather.last)):
             @pl.when(b == n)
             def _():
                 part(1)
@@ -595,16 +613,16 @@
     gather.drain(1)
     g_ref[...] = image_ref[1].astype(F32).reshape(CELLS, C)
     stages = [unit.stages() for unit in units]
-    depth = len(stages[0])
 
     def run_stages(t, first):
-        for n in range(depth):
-            ago = n - first
-            b = NB - 1 - t + (ago + 1) // 2
-
-            @pl.when((b >= 0) & (b < NB))
-            def _():
-                stages[ago % 2][n](b)
+        for n, (late, early) in enumerate(zip(PACE_LATE, PACE_EARLY)):
+            spans = [(late, 0, NB)] if late == early else [(late, 0, NB // 2), (early, NB // 2, NB)]
+            for ago, least, end in spans:
+                b = NB - 1 - t - (first - ago) // 2
+
+                @pl.when((b >= least) & (b < end))
+                def _():
+                    stages[(first - ago) % 2][n](b)
 
     def tick(t, _):
         b = NB - 1 - t
@@ -621,7 +639,7 @@
         run_stages(t, 1)
         return 0
 
-    lax.fori_loop(0, NB + depth // 2, tick, 0)
+    lax.fori_loop(0, max(2 * NB - 1 + PACE_LATE[-1], NB - 1 + PACE_EARLY[-1]) // 2 + 1, tick, 0)
 
 
 def step(heights, images, cotangent, up, down, small):

time: 190 us -> 171 us (0.900)
  Pallas kernels: 176 us -> 158 us
    pallas_call x1, Pallas kernels: 176 us -> 158 us  [step(): pl.pallas_call(step_kernel, out_shape=(jax.ShapeDtypeStruct((2, C, HID),...]
where the time goes in v4:
time: 171 us; the launch traced here: 170 us
  Pallas kernels  158 us (92%)
  local copies, waits for them, and re-layouts  11.5 us (7%)
    pallas_call x1, Pallas kernels, step(): pl.pallas_call(step_kernel, out_shape=(jax.ShapeDtypeStruct((2, C, HID),...  158 us
    unnamed x9, local copies, waits for them, and re-layouts  7.32 us

profile of v4, /device:TPU:1, one launch (start us, length us, event | category | flops | bytes accessed | tf_op | source)
XLA Modules:
  0.0 170.4 jit_solution(10351704978342422692)
XLA Ops:
  0.6 1.0 copy.24
  1.7 0.8 concatenate.6
  2.5 0.7 copy.33
  3.2 0.1 pad.12.clone
  3.3 0.8 fusion.small_in
  4.0 157.5 %shard_map.187 = (bf16[2,320,1280]{2,1,0:T(8,128)(2,1)}, bf16[2,320,1280]{2,1,0:T(8,128)(2,1)}, f32[2,64,384]{2,1,0:T(8,128)}) custom-call(s32[4]{0:T(128)} %heights_ref.1, bf16[4,1,16,16,320]{4,3,2,1,0:T(8,128)(2,1)} %images_ref.1, bf16[4,1,16,16,320]{4,3,2,1,0:T(8,128)(2,1)} %cot_ref.1, bf16[2,320,1280]{2,1,0:T(8,128)(2,1)} %bitcast.26, ...), custom_call_target="tpu_custom_call" | custom-call | flops 12000000000 | bytes 30000000 | tf_op jit(solution)/shard_map/pallas_call | solution.py:668
  161.6 1.6 fusion.1
  163.2 0.9 slice.24
  164.1 0.1 copy.26
  164.2 0.8 copy.27
  165.0 0.8 slice_bitcast_fusion
  165.8 0.6 broadcast_in_dim.14
  166.4 0.0 copy-start
  166.4 2.8 %copy.36 = bf16[2,1,320,1280]{3,2,1,0:T(8,128)(2,1)} copy(bf16[2,1,320,1280]{3,2,1,0:T(8,128)(2,1)} %bitcast.21) | data formatting | bytes 3276800
  169.3 0.0 copy-done
  169.3 1.2 copy.37
  (6 shorter events, 0.1 us)
Async XLA Ops:
  166.4 2.8 %copy-start = (bf16[2,320,1280]{2,1,0:T(8,128)(2,1)S(1)}, bf16[2,320,1280]{2,1,0:T(8,128)(2,1)}, u32[]{:S(2)}) copy-start(bf16[2,320,1280]{2,1,0:T(8,128)(2,1)} %get-tuple-element.14) | copy-start | bytes 4915204

commit v5 on v4

--- a/solution.py
+++ b/solution.py
@@ -55,7 +55,7 @@
     lax.fori_loop(0, 3, tile, 0)
 
 
-def conv_backward(shift_ref, x_ref, small_ref, b, dx_ref, dk_ref):
+def conv_backward(shift_ref, x_ref, small_ref, b, dx_ref, dk_ref, inputs):
     def tile(t, _):
         lanes = lane_tile(t)
         for half in range(2):
@@ -70,8 +70,9 @@
                     for dr in range(7):
                         i = r + dr - 3
                         if 0 <= i < SIDE:
-                            p = g * taps[dr]
-                            acc[i] = p if acc[i] is None else acc[i] + p
+                            if inputs:
+                                p = g * taps[dr]
+                                acc[i] = p if acc[i] is None else acc[i] + p
                             p = g * xs[i]
                             dks[dr] = p if dks[dr] is None else dks[dr] + p
                 for dr in range(7):
@@ -79,7 +80,7 @@
                         dk_ref[dr * 7 + dj, :, lanes] = dks[dr]
                     else:
                         dk_ref[dr * 7 + dj, :, lanes] += dks[dr]
-            for i in range(SIDE):
+            for i in range(SIDE if inputs else 0):
                 dx_ref[i, cols, lanes] = acc[i]
         return 0
 
@@ -176,14 +177,15 @@
     pad_ref[:, 8:24, 0:C] = dmixed.reshape(SIDE, SIDE, C)
 
 
-def spatial_backward(b, g_ref, w_ref, small_ref, v_ref, pad_ref, shift_ref, mix_ref, x_ref, dk_ref, sg_ref):
+def spatial_backward(b, g_ref, w_ref, small_ref, v_ref, pad_ref, shift_ref, mix_ref, x_ref, dk_ref, sg_ref, inputs):
     x_ref[:, :, 0:C] = v_ref[b].astype(F32).reshape(SIDE, SIDE, C)
     shift_columns(pad_ref, shift_ref, 11, -1)
-    conv_backward(shift_ref, x_ref, small_ref, b, mix_ref, dk_ref)
+    conv_backward(shift_ref, x_ref, small_ref, b, mix_ref, dk_ref, inputs)
     sg_ref[0:49, :] = jnp.sum(dk_ref[...], axis=1)
     for j in range(3):
         w_ref[b, SMALL + 64 * j : SMALL + 64 * j + 64, :] = sg_ref[:, 128 * j : 128 * j + 128].astype(BF)
-    g_ref[...] = (g_ref[...] + mix_ref[:, :, 0:C].reshape(CELLS, C)).astype(BF).astype(F32)
+    if inputs:
+        g_ref[...] = (g_ref[...] + mix_ref[:, :, 0:C].reshape(CELLS, C)).astype(BF).astype(F32)
 
 
 def pack_small(dw_kernel, dw_bias, gain, nbias, up_bias, down_bias, scale):
@@ -591,10 +593,10 @@
         c.wait()
     v_ref[0] = (image_ref[0].astype(F32).reshape(CELLS, C) * window_of(h)).astype(BF)
     gather.near(0)
-    gather.begin(1)
     gather.small_ones(0)
     spatial_forward(0, small_ref, v_ref, pad_ref, shift_ref, mix_ref, xhat_ref, inv_ref)
     gather.far(0)
+    gather.begin(1)
     gather.last(0)
 
     def forward(b, _):
@@ -602,7 +604,7 @@
         def _():
             spatial_forward(b, small_ref, v_ref, pad_ref, shift_ref, mix_ref, xhat_ref, inv_ref)
         products_forward(b, h, w_ref, small_ref, v_ref, act_ref, slope_ref, xhat_ref, proj_ref)
-        for n, part in ((0, gather.near), (2, gather.far), (2, gather.small_ones), (3, gather.last)):
+        for n, part in ((1, gather.near), (3, gather.far), (3, gather.small_ones), (3, gather.last)):
             @pl.when(b == n)
             def _():
                 part(1)
@@ -633,9 +635,13 @@
             products_backward(b, h, g_ref, w_ref, small_ref, pad_ref, act_ref, slope_ref, xhat_ref, inv_ref, proj_ref, sg_ref)
         run_stages(t, 0)
 
-        @pl.when(b >= 0)
-        def _():
-            spatial_backward(b, g_ref, w_ref, small_ref, v_ref, pad_ref, shift_ref, mix_ref, x_ref, dk_ref, sg_ref)
+        @pl.when(b > 0)
+        def _():
+            spatial_backward(b, g_ref, w_ref, small_ref, v_ref, pad_ref, shift_ref, mix_ref, x_ref, dk_ref, sg_ref, True)
+
+        @pl.when(b == 0)
+        def _():
+            spatial_backward(0, g_ref, w_ref, small_ref, v_ref, pad_ref, shift_ref, mix_ref, x_ref, dk_ref, sg_ref, False)
         run_stages(t, 1)
         return 0
 

time: 171 us -> 170 us (level)
  no operation moved by 1% of the time
where the time goes in v5:
time: 170 us
  Pallas kernels  157 us (92%)
  local copies, waits for them, and re-layouts  11.5 us (7%)
    pallas_call x1, Pallas kernels, step(): pl.pallas_call(step_kernel, out_shape=(jax.ShapeDtypeStruct((2, C, HID),...  157 us
    unnamed x9, local copies, waits for them, and re-layouts  7.32 us

profile of v5, /device:TPU:1, one launch (start us, length us, event | category | flops | bytes accessed | tf_op | source)
XLA Modules:
  0.0 169.8 jit_solution(10809332780411691538)
XLA Ops:
  0.6 1.0 copy.24
  1.7 0.8 concatenate.6
  2.5 0.7 copy.33
  3.2 0.1 pad.12.clone
  3.3 0.8 fusion.small_in
  4.0 156.9 %shard_map.187 = (bf16[2,320,1280]{2,1,0:T(8,128)(2,1)}, bf16[2,320,1280]{2,1,0:T(8,128)(2,1)}, f32[2,64,384]{2,1,0:T(8,128)}) custom-call(s32[4]{0:T(128)} %heights_ref.1, bf16[4,1,16,16,320]{4,3,2,1,0:T(8,128)(2,1)} %images_ref.1, bf16[4,1,16,16,320]{4,3,2,1,0:T(8,128)(2,1)} %cot_ref.1, bf16[2,320,1280]{2,1,0:T(8,128)(2,1)} %bitcast.26, ...), custom_call_target="tpu_custom_call" | custom-call | flops 12000000000 | bytes 30000000 | tf_op jit(solution)/shard_map/pallas_call | solution.py:674
  160.9 1.6 fusion.1
  162.6 0.9 slice.24
  163.5 0.1 copy.26
  163.6 0.8 copy.27
  164.4 0.8 slice_bitcast_fusion
  165.2 0.6 broadcast_in_dim.14
  165.8 0.0 copy-start
  165.8 2.8 %copy.36 = bf16[2,1,320,1280]{3,2,1,0:T(8,128)(2,1)} copy(bf16[2,1,320,1280]{3,2,1,0:T(8,128)(2,1)} %bitcast.21) | data formatting | bytes 3276800
  168.6 0.0 copy-done
  168.7 1.2 copy.37
  (6 shorter events, 0.1 us)
Async XLA Ops:
  165.8 2.8 %copy-start = (bf16[2,320,1280]{2,1,0:T(8,128)(2,1)S(1)}, bf16[2,320,1280]{2,1,0:T(8,128)(2,1)}, u32[]{:S(2)}) copy-start(bf16[2,320,1280]{2,1,0:T(8,128)(2,1)} %get-tuple-element.14) | copy-start | bytes 4915204
